TPU v7x, 32 devices: a whole 2x2x4 slice. The times are simulated.
32 devices in a mesh: tile: 8 (over y, x, core), fsdp: 4 (over z).
Axes of the slice: x: 2, y: 2, z: 4, core: 2. Of those that a mesh axis runs over, the one named last changes fastest.
Arguments:
- images: bfloat16 [4, 8, 8, 128, 320], P('fsdp', 'tile'), may hold values from -80 to 80
- tile_rows: int32 [4, 8], P('fsdp', 'tile'), may hold values from 1 to 8, 40 in all within a row
- cotangent: bfloat16 [4, 8, 8, 128, 320], P('fsdp', 'tile'), may hold values from -6 to 6
- master_weight: float32 [2880, 320], P('fsdp'), may hold values from -0.109375 to 0.109375
- norm_gain: float32 [320], replicated, may hold values from 0.5 to 1.5
- norm_bias: float32 [320], replicated, may hold values from -3 to 3
- first_moment: float32 [2880, 320], P('fsdp'), may hold values from -6 to 6
- second_moment: float32 [2880, 320], P('fsdp'), may hold values from 0.5 to 4
Outputs:
- activation: bfloat16 [4, 8, 8, 128, 320], P('fsdp', 'tile')
- image_grad: bfloat16 [4, 8, 8, 128, 320], P('fsdp', 'tile')
- weight_grad: float32 [2880, 320], P('fsdp')
- new_weight: float32 [2880, 320], P('fsdp')
- new_first: float32 [2880, 320], P('fsdp')
- new_second: float32 [2880, 320], P('fsdp')
- gain_grad: float32 [320], replicated
- bias_grad: float32 [320], replicated
Inputs may be any that keep to these rules, and one draw needn't show every extreme that they name: `tile_rows`: in each frame the 8 counts sum to 40 and the largest is exactly 8.
All inputs are finite; a program needn't handle non-finite values. No bound on the sum of `tile_rows` on one device may be relied on, other than what follows from the above.
Results may differ from a plain program's by a relative error of at most 0.027.
Values may be sent and summed in bfloat16 or wider, within the bound.
A program may use at most 64 MiB of HBM per device.

v0:
```python
import jax
import jax.numpy as jnp
from jax import lax
from jax.sharding import PartitionSpec as P

GROUPS = 32
ROWS_MEAN = 5


def extended(cells, sides, width):
    for axis, dim in sides:
        count = lax.axis_size(axis)
        ends = count - 1
        head = lax.slice_in_dim(cells, 0, width, axis=dim)
        tail = lax.slice_in_dim(cells, cells.shape[dim] - width, cells.shape[dim], axis=dim)
        cells = jnp.concatenate(
            [
                lax.ppermute(tail, axis, [(i, (i + 1) % count) for i in range(ends)]),
                cells,
                lax.ppermute(head, axis, [((i + 1) % count, i) for i in range(ends)]),
            ],
            axis=dim,
        )
    return cells


def edge_pair(source, live_count):
    first_row = source[0:1]
    last_row = lax.dynamic_slice_in_dim(source, live_count - 1, 1, 0)
    return jnp.concatenate([first_row, last_row], axis=0)


def framed(source, beside_all, live_count):
    slot_count = source.shape[0]
    zero_row = jnp.zeros_like(source[0:1])
    stacked = jnp.concatenate([beside_all[0:1], source, zero_row], axis=0)
    marker = (jnp.arange(slot_count + 2) == live_count + 1)[:, None, None]
    stacked = jnp.where(marker, beside_all[3:4], stacked)
    return jnp.pad(stacked, ((0, 0), (1, 1), (0, 0)))


def patches_of(padded, slot_count, cell_cols):
    pieces = [
        padded[row_step : row_step + slot_count, col_step : col_step + cell_cols, :]
        for row_step in range(3)
        for col_step in range(3)
    ]
    return jnp.concatenate(pieces, axis=-1).reshape(slot_count * cell_cols, -1)


def local(
    images, tile_rows, cotangent, master_weight, norm_gain, norm_bias, first_moment, second_moment
):
    slot_count, cell_cols, channels = (images.shape[2], images.shape[3], images.shape[4])
    per_group = channels // GROUPS
    tile_count = lax.axis_size("tile")
    shards = lax.axis_size("fsdp")
    population = jnp.float32(ROWS_MEAN * tile_count * cell_cols * per_group)
    live_count = tile_rows[0, 0]
    live_rows = jnp.arange(slot_count) < live_count
    cell_mask = jnp.repeat(live_rows, cell_cols).astype(jnp.float32)[:, None]

    def grouped(values):
        return jnp.sum(values.reshape(-1, GROUPS, per_group), axis=(0, 2))

    def spread(stat):
        return jnp.repeat(stat, per_group)

    source = jnp.where(live_rows[:, None, None], images[0, 0], jnp.zeros((), jnp.bfloat16))
    beside_all = extended(edge_pair(source, live_count), (("tile", 0),), 1)
    columns = patches_of(framed(source, beside_all, live_count), slot_count, cell_cols)
    gathered = lax.all_gather(master_weight.astype(jnp.bfloat16), "fsdp", axis=0, tiled=True)
    mixed = jnp.dot(columns, gathered, preferred_element_type=jnp.float32)
    group_mean = lax.psum(grouped(mixed * cell_mask), "tile") / population
    centered = (mixed - spread(group_mean)) * cell_mask
    variance = lax.psum(grouped(centered * centered), "tile") / population
    inverse = lax.rsqrt(variance + 1e-05)
    normed = (mixed - spread(group_mean)) * spread(inverse)
    shifted = normed * norm_gain + norm_bias
    gate_value = jax.nn.sigmoid(shifted)
    activation = (shifted * gate_value * cell_mask).astype(jnp.bfloat16).reshape(images.shape)
    upstream = cotangent[0, 0].reshape(-1, channels).astype(jnp.float32) * cell_mask
    dshift = upstream * gate_value * (1.0 + shifted * (1.0 - gate_value))
    scaled = dshift * norm_gain
    delta_sum, cross_sum = lax.psum((grouped(scaled), grouped(scaled * normed)), "tile")
    gain_total, bias_total = lax.psum(
        (jnp.sum(dshift * normed, axis=0), jnp.sum(dshift, axis=0)), ("tile", "fsdp")
    )
    norm_scale = jnp.float32(shards * ROWS_MEAN * tile_count * cell_cols) ** (-0.5)
    pre_grad = spread(inverse) * (
        scaled - spread(delta_sum / population) - normed * spread(cross_sum / population)
    )
    pre_grad = (pre_grad * cell_mask).astype(jnp.bfloat16)
    grad_field = pre_grad.reshape(slot_count, cell_cols, channels)
    grad_around = extended(edge_pair(grad_field, live_count), (("tile", 0),), 1)
    grad_columns = patches_of(framed(grad_field, grad_around, live_count), slot_count, cell_cols)
    flipped = (
        gathered.reshape(9, channels, channels)[::-1]
        .transpose(0, 2, 1)
        .reshape(9 * channels, channels)
    )
    image_grad = (
        (jnp.dot(grad_columns, flipped, preferred_element_type=jnp.float32) * cell_mask)
        .astype(jnp.bfloat16)
        .reshape(images.shape)
    )
    full_grad = lax.psum(
        lax.dot_general(
            columns, pre_grad, (((0,), (0,)), ((), ())), preferred_element_type=jnp.float32
        ).astype(jnp.bfloat16),
        "tile",
    )
    grad_shard = lax.psum_scatter(full_grad, "fsdp", scatter_dimension=0, tiled=True).astype(
        jnp.float32
    )
    weight_grad = grad_shard * norm_scale
    new_first = 0.9 * first_moment + 0.1 * weight_grad
    new_second = 0.999 * second_moment + 0.001 * weight_grad * weight_grad
    first_fix = new_first / (1.0 - 0.9**10)
    second_fix = new_second / (1.0 - 0.999**10)
    new_weight = master_weight - 0.01 * first_fix / (jnp.sqrt(second_fix) + 1e-08)
    return (
        activation,
        image_grad,
        weight_grad,
        new_weight,
        new_first,
        new_second,
        gain_total * norm_scale,
        bias_total * norm_scale,
    )


def solution(mesh):
    placed = (
        P("fsdp", "tile", None, None, None),
        P("fsdp", "tile"),
        P("fsdp", "tile", None, None, None),
        P("fsdp", None),
        P(),
        P(),
        P("fsdp", None),
        P("fsdp", None),
    )
    return jax.shard_map(
        local,
        mesh=mesh,
        in_specs=placed,
        out_specs=(
            P("fsdp", "tile", None, None, None),
            P("fsdp", "tile", None, None, None),
            P("fsdp", None),
            P("fsdp", None),
            P("fsdp", None),
            P("fsdp", None),
            P(),
            P(),
        ),
        check_vma=False,
    )
```

profile of v0, /device:TPU:1, one launch (start us, length us, event | category | flops | bytes accessed | tf_op | source)
XLA Modules:
  0.0 263.0 jit_solution(1942681254880703290)
XLA Ops:
  7.2 2.1 convert_bitcast_fusion
  10.3 2.0 collective-permute-start
  12.2 4.5 %collective-permute-start.1 = (bf16[1,128,320]{1,2,0:T(8,128)(2,1)S(1)}, bf16[1,128,320]{1,2,0:T(8,128)(2,1)S(1)}, u32[]{:S(2)}, u32[]{:S(2)}) collective-permute-start(bf16[1,128,320]{1,2,0:T(8,128)(2,1)S(1)} %get-tuple-element.47), channel_id=1, source_target_pairs={{0,4},{4,8},{8,12},{12,16},{16,20},{20,24},{24,28},{1,5},{5,9},{9,... | collective-permute-start | bytes 245768 | tf_op jit(solution)/shard_map/ppermute | solution.py:18
  16.7 1.5 copy.33
  18.6 1.1 fusion.7
  19.7 1.0 slice_dynamic-update-slice_fusion.5
  20.7 1.1 fusion.8
  21.8 1.1 fusion.9
  22.9 1.0 slice_dynamic-update-slice_fusion.4
  23.9 1.1 fusion.10
  25.0 1.1 fusion.11
  26.1 1.0 slice_dynamic-update-slice_fusion.3
  27.0 1.1 fusion.12
  28.1 8.4 %copy.31 = bf16[8,128,2880]{2,1,0:T(8,128)(2,1)} copy(bf16[8,128,2880]{1,2,0:T(8,128)(2,1)} %fusion.12) | data formatting | bytes 11796480 | tf_op jit(solution)/shard_map/concatenate | solution.py:48
  36.6 19.3 %all-gather.3.cloned.1.call-done = bf16[4,720,320]{1,2,0:T(8,128)(2,1)} async-done(((bf16[1,720,320]{1,2,0:T(8,128)(2,1)}), bf16[4,720,320]{1,2,0:T(8,128)(2,1)}) %all-gather.3.cloned.1.call-update) | async-done | bytes 1843216 | tf_op jit(solution)/shard_map/all_gather | solution.py:72
  55.8 3.1 %copy.32 = bf16[4,720,320]{1,0,2:T(4,128)(2,1)S(1)} copy(bf16[4,720,320]{1,2,0:T(8,128)(2,1)} %all-gather.3.cloned.1.call-done) | data formatting | bytes 3686400 | tf_op jit(solution)/shard_map/all_gather | solution.py:72
  58.9 2.6 reshape.78
  61.5 5.6 %multiply_reduce_fusion.3 = (f32[320]{0:T(512)S(1)}, f32[1024,320]{0,1:T(8,128)S(1)}) fusion(f32[1024]{0:T(1024)S(1)} %broadcast_bitcast_fusion, bf16[1024,2880]{1,0:T(8,128)(2,1)} %bitcast.61, bf16[2880,320]{0,1:T(8,128)(2,1)} %reshape.78), kind=kOutput, calls=%fused_computation.29 | convolution fusion | flops 1888091904 | bytes 9057536 | tf_op jit(solution)/shard_map/dot_general | solution.py:73
  67.3 11.8 %psum.49 = f32[32]{0:T(128)S(1)} all-reduce(f32[32]{0:T(128)S(1)} %reduce_sum.67), channel_id=1, replica_groups=mesh['tile'=8,'fsdp'=4] {'tile'}, use_global_device_ids=true, to_apply=%region_2.3 | all-reduce | flops 32 | bytes 256 | tf_op jit(solution)/shard_map/psum | solution.py:74
  79.9 13.6 %psum.50 = f32[32]{0:T(128)S(1)} all-reduce(f32[32]{0:T(128)S(1)} %reduce_sum.73), channel_id=1, replica_groups=mesh['tile'=8,'fsdp'=4] {'tile'}, use_global_device_ids=true, to_apply=%region_5.6 | all-reduce | flops 32 | bytes 256 | tf_op jit(solution)/shard_map/psum | solution.py:76
  93.8 3.5 %multiply_reduce_fusion = (f32[320]{0:T(512)S(1)}, f32[320]{0:T(512)S(1)}, f32[320]{0:T(512)S(1)}, f32[320]{0:T(512)S(1)}, f32[1024,320]{0,1:T(8,128)S(1)}, /*index=5*/bf16[40,8,8,128]{3,1,2,0:T(8,128)(2,1)}) fusion(f32[1024,320]{0,1:T(8,128)S(1)} %get-tuple-element.49, f32[320]{0:T(512)S(1)} %mul.152, f32[320]{0:T(512)S(1)} %sub.38, f32[320]{0:T(512)S(1)} %copy-done.7, ...), kind=kLoop, calls=%fused_computation.22 | loop fusion | flops 7535360 | bytes 4601856 | tf_op jit(solution)/shard_map/reduce_sum | solution.py:87
  97.7 12.0 %all-reduce.3 = (f32[32]{0:T(128)S(1)}, f32[32]{0:T(128)S(1)}) all-reduce(f32[32]{0:T(128)S(1)} %reduce_sum.93, f32[32]{0:T(128)S(1)} %reduce_sum.90), channel_id=1, replica_groups=mesh['tile'=8,'fsdp'=4] {'tile'}, use_global_device_ids=true, to_apply=%region_11.12 | all-reduce | flops 64 | bytes 512 | tf_op jit(solution)/shard_map/psum | solution.py:85
  110.1 0.8 multiply_convert_fusion
  110.9 4.9 %convolution_convert_fusion = bf16[2880,320]{0,1:T(8,128)(2,1)S(1)} fusion(bf16[1024,320]{0,1:T(8,128)(2,1)S(1)} %multiply_convert_fusion, bf16[1024,2880]{1,0:T(8,128)(2,1)} %bitcast.62), kind=kOutput, calls=%fused_computation | convolution fusion | flops 1888358400 | bytes 8396800 | tf_op jit(solution)/shard_map/dot_general | solution.py:108
  115.8 2.7 %copy.41 = bf16[2880,320]{1,0:T(8,128)(2,1)} copy(bf16[2880,320]{0,1:T(8,128)(2,1)S(1)} %convolution_convert_fusion) | data formatting | bytes 3686400
  119.3 1.9 collective-permute-start.3
  121.9 3.0 %collective-permute-start.2 = (bf16[1,128,320]{1,2,0:T(8,128)(2,1)}, bf16[1,128,320]{1,2,0:T(8,128)(2,1)S(1)}, u32[]{:S(2)}, u32[]{:S(2)}) collective-permute-start(bf16[1,128,320]{1,2,0:T(8,128)(2,1)} %slice_bitcast_fusion), channel_id=1, source_target_pairs={{4,0},{8,4},{12,8},{16,12},{20,16},{24,20},{28,24},{5,1},{9,5},{13... | collective-permute-start | bytes 245768 | tf_op jit(solution)/shard_map/ppermute | solution.py:20
  124.9 3.0 %copy.37 = bf16[4,720,320]{2,1,0:T(8,128)(2,1)S(1)} copy(bf16[4,720,320]{1,2,0:T(8,128)(2,1)} %all-gather.3.cloned.1.call-done) | data formatting | bytes 3686400 | tf_op jit(solution)/shard_map/all_gather | solution.py:72
  128.0 40.6 %all-reduce.2 = (f32[320]{0:T(512)S(1)}, f32[320]{0:T(512)S(1)}) all-reduce(f32[320]{0:T(512)S(1)} %get-tuple-element.32, f32[320]{0:T(512)S(1)} %get-tuple-element.35), channel_id=1, replica_groups=mesh['tile'=8,'fsdp'=4] {'tile','fsdp'}, use_global_device_ids=true, to_apply=%region_15.16 | all-reduce | flops 640 | bytes 5120 | tf_op jit(solution)/shard_map/psum | solution.py:86
  169.2 1.6 reverse_bitcast_fusion
  170.8 4.3 %copy.38 = bf16[9,320,320]{2,1,0:T(8,128)(2,1)} copy(bf16[9,320,320]{1,2,0:T(8,128)(2,1)} %reverse_bitcast_fusion) | data formatting | bytes 3686400 | tf_op jit(solution)/shard_map/transpose | solution.py:99
  175.2 0.9 copy.39
  176.2 1.1 maximum_select_fusion.1
  177.3 1.1 fusion.13
  178.4 1.0 slice_dynamic-update-slice_fusion.2
  179.4 1.1 fusion.14
  180.5 1.1 fusion.15
  181.6 1.0 slice_dynamic-update-slice_fusion.1
  182.6 1.1 fusion.16
  183.7 1.1 fusion.17
  184.8 1.0 slice_dynamic-update-slice_fusion
  185.7 1.1 fusion.18
  186.8 8.6 %copy.36 = bf16[8,128,2880]{2,1,0:T(8,128)(2,1)} copy(bf16[8,128,2880]{1,2,0:T(8,128)(2,1)} %fusion.18) | data formatting | bytes 11796480 | tf_op jit(solution)/shard_map/concatenate | solution.py:48
  195.4 2.1 copy.42
  197.5 5.0 %fusion.3 = bf16[40,8,8,128]{3,1,2,0:T(8,128)(2,1)S(1)} fusion(bf16[1024,2880]{1,0:T(8,128)(2,1)} %bitcast.63, bf16[2880,320]{1,0:T(8,128)(2,1)S(1)} %bitcast.67, f32[1024]{0:T(1024)S(1)} %broadcast_bitcast_fusion), kind=kOutput, calls=%fused_computation.30 | convolution fusion | flops 1888092160 | bytes 8400896 | tf_op jit(solution)/shard_map/dot_general | solution.py:103
  202.7 0.9 copy.40
  203.7 49.4 %all-reduce.6.cloned.1.call-done = bf16[720,320]{0,1:T(8,128)(2,1)} async-done(((bf16[720,320]{0,1:T(8,128)(2,1)}), bf16[720,320]{0,1:T(8,128)(2,1)}) %all-reduce.6.cloned.1.call-update) | async-done | bytes 460816 | tf_op jit(solution)/shard_map/psum | solution.py:107
  253.0 3.5 %divide_subtract_fusion = (f32[720,320]{0,1:T(8,128)}, f32[720,320]{0,1:T(8,128)}, f32[720,320]{0,1:T(8,128)}, f32[720,320]{0,1:T(8,128)}) fusion(f32[720,320]{0,1:T(8,128)S(1)} %copy-done, bf16[720,320]{0,1:T(8,128)(2,1)} %all-reduce.6.cloned.1.call-done, f32[720,320]{0,1:T(8,128)S(1)} %copy-done.3, f32[720,320]{0,1:T(8,128)S(1)} %copy-done.4), kind=kLoop, calls=%fused_computation.36 | loop fusion | flops 3225600 | bytes 6912000 | tf_op jit(solution)/shard_map/sub | solution.py:121
  (63 shorter events, 4.9 us)
Async XLA Ops:
  7.2 2.9 %copy-start.5 = (bf16[1,1,8,128,320]{3,4,2,1,0:T(8,128)(2,1)S(1)}, bf16[1,1,8,128,320]{3,4,2,1,0:T(8,128)(2,1)}, u32[]{:S(2)}) copy-start(bf16[1,1,8,128,320]{3,4,2,1,0:T(8,128)(2,1)} %param.8) | copy-start | bytes 1966084
  7.2 9.5 %copy-start.6 = (bf16[1,1,8,128,320]{3,4,2,1,0:T(8,128)(2,1)S(1)}, bf16[1,1,8,128,320]{3,4,2,1,0:T(8,128)(2,1)}, u32[]{:S(2)}) copy-start(bf16[1,1,8,128,320]{3,4,2,1,0:T(8,128)(2,1)} %param.10) | copy-start | bytes 1966084
  7.2 48.7 %all-gather.3.cloned.1.call-start = ((), (), s32[]{:S(2)}) async-start(), calls=%async_computation.2 | async-start | bytes 2457600 | tf_op jit(solution)/shard_map/all_gather | solution.py:72
  9.4 186.1 %reduce-scatter.4.cloned.1.call-start = ((), (), s32[]{:S(2)}) async-start(), calls=%async_computation.3 | async-start | bytes 2764800
  10.3 8.1 %collective-permute-start = (bf16[1,128,320]{1,2,0:T(8,128)(2,1)S(1)}, bf16[1,128,320]{1,2,0:T(8,128)(2,1)S(1)}, u32[]{:S(2)}, u32[]{:S(2)}) collective-permute-start(bf16[1,128,320]{1,2,0:T(8,128)(2,1)S(1)} %get-tuple-element.46), channel_id=1, source_target_pairs={{4,0},{8,4},{12,8},{16,12},{20,16},{24,20},{28,24},{5,1},{9,5},{13... | collective-permute-start | bytes 245768 | tf_op jit(solution)/shard_map/ppermute | solution.py:20
  12.2 6.1 %collective-permute-start.1 = (bf16[1,128,320]{1,2,0:T(8,128)(2,1)S(1)}, bf16[1,128,320]{1,2,0:T(8,128)(2,1)S(1)}, u32[]{:S(2)}, u32[]{:S(2)}) collective-permute-start(bf16[1,128,320]{1,2,0:T(8,128)(2,1)S(1)} %get-tuple-element.47), channel_id=1, source_target_pairs={{0,4},{4,8},{8,12},{12,16},{16,20},{20,24},{24,28},{1,5},{5,9},{9,... | collective-permute-start | bytes 245768 | tf_op jit(solution)/shard_map/ppermute | solution.py:18
  61.5 32.3 %copy-start.7 = (f32[320]{0:T(512)S(1)}, f32[320]{0:T(512)}, u32[]{:S(2)}) copy-start(f32[320]{0:T(512)} %param.12) | copy-start | bytes 3844
  61.5 32.3 %copy-start.8 = (f32[320]{0:T(512)S(1)}, f32[320]{0:T(512)}, u32[]{:S(2)}) copy-start(f32[320]{0:T(512)} %param.13) | copy-start | bytes 3844
  118.5 134.5 %all-reduce.6.cloned.1.call-start = ((), (), s32[]{:S(2)}) async-start(), calls=%async_computation.1 | async-start | bytes 983040 | tf_op jit(solution)/shard_map/psum | solution.py:107
  119.3 56.8 %collective-permute-start.3 = (bf16[1,128,320]{1,2,0:T(8,128)(2,1)}, bf16[1,128,320]{1,2,0:T(8,128)(2,1)}, u32[]{:S(2)}, u32[]{:S(2)}) collective-permute-start(bf16[1,128,320]{1,2,0:T(8,128)(2,1)} %constant_dynamic-slice_fusion), channel_id=1, source_target_pairs={{0,4},{4,8},{8,12},{12,16},{16,20},{20,24},{24,28},{1,5},{5,9},{9,... | collective-permute-start | bytes 245768 | tf_op jit(solution)/shard_map/ppermute | solution.py:18
  121.9 54.3 %collective-permute-start.2 = (bf16[1,128,320]{1,2,0:T(8,128)(2,1)}, bf16[1,128,320]{1,2,0:T(8,128)(2,1)S(1)}, u32[]{:S(2)}, u32[]{:S(2)}) collective-permute-start(bf16[1,128,320]{1,2,0:T(8,128)(2,1)} %slice_bitcast_fusion), channel_id=1, source_target_pairs={{4,0},{8,4},{12,8},{16,12},{20,16},{24,20},{28,24},{5,1},{9,5},{13... | collective-permute-start | bytes 245768 | tf_op jit(solution)/shard_map/ppermute | solution.py:20
  170.8 4.3 %copy-start.1 = (bf16[40,8,8,128]{3,1,2,0:T(8,128)(2,1)S(1)}, bf16[40,8,8,128]{3,1,2,0:T(8,128)(2,1)}, u32[]{:S(2)}) copy-start(bf16[40,8,8,128]{3,1,2,0:T(8,128)(2,1)} %get-tuple-element.45) | copy-start | bytes 1966084
  186.8 10.7 %copy-start.2 = (bf16[9,320,320]{2,1,0:T(8,128)(2,1)S(1)}, bf16[9,320,320]{2,1,0:T(8,128)(2,1)}, u32[]{:S(2)}) copy-start(bf16[9,320,320]{2,1,0:T(8,128)(2,1)} %copy.38) | copy-start | bytes 5529604
  197.5 55.5 %copy-start.4 = (f32[720,320]{0,1:T(8,128)S(1)}, f32[720,320]{0,1:T(8,128)}, u32[]{:S(2)}) copy-start(f32[720,320]{0,1:T(8,128)} %param.15) | copy-start | bytes 2764804
  202.6 50.5 %copy-start = (f32[720,320]{0,1:T(8,128)S(1)}, f32[720,320]{0,1:T(8,128)}, u32[]{:S(2)}) copy-start(f32[720,320]{0,1:T(8,128)} %param.11) | copy-start | bytes 2764804
  202.6 50.5 %copy-start.3 = (f32[720,320]{0,1:T(8,128)S(1)}, f32[720,320]{0,1:T(8,128)}, u32[]{:S(2)}) copy-start(f32[720,320]{0,1:T(8,128)} %param.14) | copy-start | bytes 2764804
Sparse Core Ops, SparseCore 0:
  10.2 45.6 all-gather.2
  118.6 43.6 reduce-scatter.3
  197.6 55.3 all-reduce.5
where the time goes:
time: 265 us; the launch traced here: 263 us
  blocking collectives  78.1 us (29%)
  waiting for transfers between devices  68.7 us (26%)
  local copies, waits for them, and re-layouts  61.8 us (23%)
  matrix products  15.6 us (6%)
  between operations  14.7 us (6%)
  other arithmetic  12.8 us (5%)
  starting transfers between devices  11.5 us (4%)
    psum x1, waiting for transfers between devices, local(): lax.psum(lax.dot_general(columns, pre_grad, (((0,), (0,)), ((), ())), pre...  49.4 us
    psum x1, blocking collectives, local(): lax.psum((jnp.sum(dshift * normed, axis=0), jnp.sum(dshift, axis=0)), ('t...  40.6 us
    unnamed x41, local copies, waits for them, and re-layouts  26.3 us
    all_gather x1, waiting for transfers between devices, local(): lax.all_gather(master_weight.astype(jnp.bfloat16), 'fsdp', axis=0, tiled=...  19.3 us
    concatenate x4, local copies, waits for them, and re-layouts, patches_of(): return jnp.concatenate(pieces, axis=-1).reshape(slot_count * cell_cols, -1)  19.2 us
    psum x1, blocking collectives, local(): variance = lax.psum(grouped(centered * centered), 'tile') / population  13.6 us
    psum x1, blocking collectives, local(): lax.psum((grouped(scaled), grouped(scaled * normed)), 'tile')  12 us
    psum x1, blocking collectives, local(): group_mean = lax.psum(grouped(mixed * cell_mask), 'tile') / population  11.8 us
  transfers between devices with their start and end apart: 7, of which 2 were waited for; matrix products, arithmetic and copies ran while one was open for 22% of the time, Pallas kernels for 0%

commit v1 on v0

v1 whole, which is shorter than its diff:
```python
import functools

import jax
import jax.numpy as jnp
from jax import lax
from jax.experimental import pallas as pl
from jax.experimental.pallas import tpu as pltpu
from jax.sharding import PartitionSpec as P

GROUPS = 32
ROWS_MEAN = 5
MESH = pl.DeviceIdType.MESH
F32 = jnp.float32
BF16 = jnp.bfloat16


def row_pieces(total, shards, shard, part, block):
    found = []
    for f in range(shards):
        for p in range(-(-shard // part)):
            low, high = f * shard + p * part, f * shard + min(shard, (p + 1) * part)
            at = low
            while at < high:
                end = min(high, (at // block + 1) * block)
                found.append((f, p, at - low, end - at, at // block, at % block))
                at = end
    return found


def kernel(
    tiles, shards, part,
    rows_ref, x_ref, ct_ref, w_ref, gain_ref, bias_ref, m1_ref, m2_ref, same_ref,
    act_ref, ig_ref, wg_ref, nw_ref, n1_ref, n2_ref, gg_ref, bg_ref,
    gath, wb, wt, wide, xcat, xcat_t, cat, y0, y1, y2, up, g0, g1, g2,
    hs, hr, hs2, hr2, st, sd, sz,
    dwbuf, dwf, sbuf, pbuf, qbuf, zbuf, rbuf, fbuf,
    z_s, z_r, p_s, p_r, s_s, s_r, h_s, h_r, h2_s, h2_r, st_s, st_r, sd_s, sd_r, sz_s, sz_r,
    b_s, b_r, q_s, q_r, r_s, r_r, f_s, f_r, e_s, e_r,
):
    slots, cols, chan = x_ref.shape
    cells = slots * cols
    shard = w_ref.shape[0]
    total = shards * shard
    chips = tiles // 2
    t = lax.axis_index("tile")
    f = lax.axis_index("fsdp")
    ch, c = t // 2, t % 2
    sibling = ch * 2 + (1 - c)
    live = rows_ref[0, 0]
    aligned = shard % 16 == 0
    sent = []

    def peer_chip(j):
        return lax.rem(ch + j, chips)

    def from_chip(j):
        return lax.rem(ch + chips - j, chips)

    def copy(src, dst, send, recv, to_tile, to_shard):
        return pltpu.make_async_remote_copy(
            src_ref=src, dst_ref=dst, send_sem=send, recv_sem=recv,
            device_id=(to_tile, to_shard), device_id_type=MESH,
        )

    def push(*args):
        made = copy(*args)
        made.start()
        sent.append(made)

    barrier = pltpu.get_barrier_semaphore()
    for j in range(1, tiles):
        pl.semaphore_signal(barrier, inc=1, device_id=(lax.rem(t + j, tiles), f), device_id_type=MESH)
    for k in range(1, shards):
        pl.semaphore_signal(barrier, inc=1, device_id=(t, lax.rem(f + k, shards)), device_id_type=MESH)

    for p in range(tiles):
        low, high = p * part, min(shard, (p + 1) * part)
        if high <= low:
            gath[f, p] = jnp.zeros((part, chan), BF16)
        else:
            rows = w_ref[low:high, :]
            if high - low < part:
                rows = jnp.concatenate([rows, jnp.zeros((part - high + low, chan), F32)], axis=0)
            gath[f, p] = rows.astype(BF16)
    hs[0] = x_ref[0]
    hs[1] = x_ref[jnp.clip(live - 1, 0, slots - 1)]
    pl.semaphore_wait(barrier, tiles + shards - 2)

    for k in range(1, shards):
        push(gath.at[f, t], gath.at[f, t], z_s.at[k - 1], z_r.at[k - 1], t, lax.rem(f + k, shards))

    def halo_copies(src, dst, send, recv):
        up_copy = copy(src.at[0], dst.at[1], send.at[0], recv.at[1], lax.rem(t + tiles - 1, tiles), f)
        down_copy = copy(src.at[1], dst.at[0], send.at[1], recv.at[0], lax.rem(t + 1, tiles), f)
        return up_copy, down_copy

    def halo_start(src, dst, send, recv):
        up_copy, down_copy = halo_copies(src, dst, send, recv)

        @pl.when(t > 0)
        def _():
            up_copy.start()

        @pl.when(t == 0)
        def _():
            dst[0] = jnp.zeros((cols, chan), BF16)

        @pl.when(t < tiles - 1)
        def _():
            down_copy.start()

        @pl.when(t == tiles - 1)
        def _():
            dst[1] = jnp.zeros((cols, chan), BF16)

    def halo_wait(src, dst, send, recv):
        up_copy, down_copy = halo_copies(src, dst, send, recv)

        @pl.when(t > 0)
        def _():
            up_copy.wait_send()
            down_copy.wait_recv()

        @pl.when(t < tiles - 1)
        def _():
            down_copy.wait_send()
            up_copy.wait_recv()

    halo_start(hs, hr, h_s, h_r)

    for k in range(1, shards):
        fs = lax.rem(f + shards - k, shards)
        block = gath.at[fs, t]
        copy(block, block, z_s.at[k - 1], z_r.at[k - 1], t, f).wait_recv()
        for j in range(1, chips):
            push(block, block, p_s.at[k - 1, j - 1], p_r.at[k - 1, j - 1], peer_chip(j) * 2 + c, f)
        push(block, block, s_s.at[k - 1, 0], s_r.at[k - 1, 0], sibling, f)

    halo_wait(hs, hr, h_s, h_r)
    below = hr[1].astype(F32)

    def is_live(r):
        return (r < live).astype(F32)

    def is_end(r):
        return (r == live).astype(F32)

    for j in range(slots + 2):
        if j == 0:
            value = hr[0].astype(F32)
        elif j <= slots:
            value = x_ref[j - 1].astype(F32) * is_live(j - 1) + below * is_end(j - 1)
        else:
            value = below * is_end(slots)
        flat, turned = value.astype(BF16), value.T.astype(BF16)
        for a in range(3):
            r = j - a
            if 0 <= r < slots:
                xcat[r * cols:(r + 1) * cols, a * chan:(a + 1) * chan] = flat
                xcat_t[a * chan:(a + 1) * chan, r * cols:(r + 1) * cols] = turned

    for k in range(1, shards):
        fs = lax.rem(f + shards - k, shards)
        for j in range(1, chips):
            block = gath.at[fs, from_chip(j) * 2 + c]
            copy(block, block, p_s.at[k - 1, j - 1], p_r.at[k - 1, j - 1], t, f).wait_recv()
            push(block, block, s_s.at[k - 1, j], s_r.at[k - 1, j], sibling, f)
    for k in range(1, shards):
        fs = lax.rem(f + shards - k, shards)
        for j in range(chips):
            block = gath.at[fs, from_chip(j) * 2 + (1 - c)]
            copy(block, block, s_s.at[k - 1, j], s_r.at[k - 1, j], sibling, f).wait_recv()

    pieces = row_pieces(total, shards, shard, part, chan)
    if aligned:
        for fi, p, low, size, tap, at in pieces:
            a, b = tap // 3, tap % 3
            wb[b, a * chan + at:a * chan + at + size, :] = gath[fi, p, low:low + size, :]
    else:
        for fi in range(shards):
            for p in range(-(-shard // part)):
                size = min(shard - p * part, part)
                dwf[fi * shard + p * part:fi * shard + p * part + size, :] = (
                    gath[fi, p].astype(F32)[:size]
                )
        for tap in range(9):
            a, b = tap // 3, tap % 3
            wb[b, a * chan:(a + 1) * chan, :] = dwf[tap * chan:(tap + 1) * chan, :].astype(BF16)

    half = cells // 2

    def three(source, weights, order):
        @pl.loop(0, 2)
        def _(h):
            at = pl.ds(pl.multiple_of(h * half, half), half)
            left = source[at, :]
            for b, into in zip(order, (y0, y1, y2)):
                into[at, :] = jnp.dot(left, weights[b], preferred_element_type=F32)

    column = lax.broadcasted_iota(jnp.int32, (cols, chan), 0)

    def later(rows):
        return jnp.where(column == 0, 0.0, pltpu.roll(rows, 1, 0))

    def earlier(rows):
        return jnp.where(column == cols - 1, 0.0, pltpu.roll(rows, cols - 1, 0))

    def span(r):
        return pl.ds(pl.multiple_of(r * cols, cols), cols)

    def group_sum(row):
        return jnp.dot(row, same_ref[...], precision=lax.Precision.HIGHEST, preferred_element_type=F32)

    three(xcat, wb, (0, 1, 2))

    def mix(r, sums):
        rows = y1[span(r), :] + later(y0[span(r), :]) + earlier(y2[span(r), :])
        y1[span(r), :] = rows
        return sums + jnp.sum(rows, axis=0, keepdims=True) * is_live(r)

    zero_row = jnp.zeros((1, chan), F32)
    own_count = live.astype(F32) * (cols * (chan // GROUPS))
    count_row = jnp.zeros((1, chan), F32) + own_count
    own_mean = group_sum(lax.fori_loop(0, slots, mix, zero_row)) / count_row

    def squares(r, sums):
        off = y1[span(r), :] - own_mean
        return sums + jnp.sum(off * off, axis=0, keepdims=True) * is_live(r)

    own_square = group_sum(lax.fori_loop(0, slots, squares, zero_row))

    def tile_share(buffer, send, recv):
        for j in range(1, tiles):
            push(buffer.at[t], buffer.at[t], send.at[j - 1], recv.at[j - 1], lax.rem(t + j, tiles), f)

    def tile_wait(buffer, send, recv):
        for j in range(1, tiles):
            block = buffer.at[lax.rem(t + tiles - j, tiles)]
            copy(block, block, send.at[j - 1], recv.at[j - 1], t, f).wait_recv()

    st[t] = jnp.concatenate(
        [own_mean, own_square, count_row, jnp.zeros((5, chan), F32)], axis=0
    )
    tile_share(st, st_s, st_r)

    for tap in range(9):
        a, b = tap // 3, tap % 3
        block = wb[b, a * chan:(a + 1) * chan, :].astype(F32)
        wt[b, a * chan:(a + 1) * chan, :] = block.T.astype(BF16)

    tile_wait(st, st_s, st_r)
    population = float(ROWS_MEAN * tiles * cols * (chan // GROUPS))
    mean = zero_row
    for i in range(tiles):
        mean = mean + st[i, 0:1, :] * st[i, 2:3, :]
    mean = mean / population
    spread = zero_row
    for i in range(tiles):
        apart = st[i, 0:1, :] - mean
        spread = spread + st[i, 1:2, :] + st[i, 2:3, :] * apart * apart
    inverse = lax.rsqrt(spread / population + 1e-05)
    gain, bias = gain_ref[...], bias_ref[...]

    def gate(r, sums):
        gains, biases = sums
        mask = is_live(r)
        normed = (y1[span(r), :] - mean) * inverse
        shifted = normed * gain + bias
        s = jax.nn.sigmoid(shifted)
        act_ref[r] = (shifted * s * mask).astype(BF16)
        dshift = ct_ref[r].astype(F32) * mask * s * (1.0 + shifted * (1.0 - s))
        y1[span(r), :] = normed
        up[span(r), :] = dshift
        return (
            gains + jnp.sum(dshift * normed, axis=0, keepdims=True),
            biases + jnp.sum(dshift, axis=0, keepdims=True),
        )

    own_gain, own_bias = lax.fori_loop(0, slots, gate, (zero_row, zero_row))
    sd[t] = jnp.concatenate([own_gain, own_bias, jnp.zeros((6, chan), F32)], axis=0)
    tile_share(sd, sd_s, sd_r)
    tile_wait(sd, sd_s, sd_r)
    frame = sd[0]
    for i in range(1, tiles):
        frame = frame + sd[i]
    sz[f] = frame
    for k in range(1, shards):
        push(sz.at[f], sz.at[f], sz_s.at[k - 1], sz_r.at[k - 1], t, lax.rem(f + k, shards))
    delta = group_sum(frame[1:2] * gain) / population
    cross = group_sum(frame[0:1] * gain) / population

    @pl.loop(0, slots)
    def _(r):
        grad = inverse * (up[span(r), :] * gain - delta - y1[span(r), :] * cross) * is_live(r)
        kept = grad.astype(BF16)
        grad = kept.astype(F32)
        g1[r] = kept
        g0[span(r), :] = earlier(grad).astype(BF16)
        g2[span(r), :] = later(grad).astype(BF16)

    hs2[0] = g1[0]
    hs2[1] = g1[jnp.clip(live - 1, 0, slots - 1)]
    halo_start(hs2, hr2, h2_s, h2_r)

    for b in range(3):
        right = g1[...].reshape(cells, chan) if b == 1 else (g0 if b == 0 else g2)[...]
        wide[...] = jnp.dot(xcat_t[...], right, preferred_element_type=F32)
        if aligned:
            for fi, p, low, size, tap, at in pieces:
                if tap % 3 == b:
                    a = tap // 3
                    dwbuf[fi, p // 2, p % 2, low:low + size, :] = wide[
                        a * chan + at:a * chan + at + size, :
                    ].astype(BF16)
        else:
            for a in range(3):
                dwf[(3 * a + b) * chan:(3 * a + b + 1) * chan, :] = wide[a * chan:(a + 1) * chan, :]
    for fi in range(shards):
        for p in range(tiles):
            low, high = p * part, min(shard, (p + 1) * part)
            if high <= low:
                dwbuf[fi, p // 2, p % 2] = jnp.zeros((part, chan), BF16)
            elif not aligned:
                rows = dwf[fi * shard + low:fi * shard + high, :]
                if high - low < part:
                    rows = jnp.concatenate([rows, jnp.zeros((part - high + low, chan), F32)], axis=0)
                dwbuf[fi, p // 2, p % 2] = rows.astype(BF16)
            elif high - low < part:
                dwbuf[fi, p // 2, p % 2, high - low:part, :] = jnp.zeros((part - high + low, chan), BF16)

    order = list(range(1, shards)) + [0]
    for k in order:
        fd = lax.rem(f + k, shards)
        push(dwbuf.at[fd, :, 1 - c], sbuf.at[k], b_s.at[k], b_r.at[k], sibling, f)
    for k in order:
        fd = lax.rem(f + k, shards)
        copy(sbuf.at[k], sbuf.at[k], b_s.at[k], b_r.at[k], sibling, f).wait_recv()
        for j in range(1, chips):
            to = peer_chip(j)
            pbuf[k, j - 1] = (dwbuf[fd, to, c].astype(F32) + sbuf[k, to].astype(F32)).astype(BF16)
            push(pbuf.at[k, j - 1], qbuf.at[k, j - 1], q_s.at[k, j - 1], q_r.at[k, j - 1], to * 2 + c, f)

    halo_wait(hs2, hr2, h2_s, h2_r)
    grad_below = hr2[1].astype(F32)
    for j in range(slots + 2):
        if j == 0:
            flat = hr2[0]
        elif j <= slots:
            flat = (g1[j - 1].astype(F32) + grad_below * is_end(j - 1)).astype(BF16)
        else:
            flat = (grad_below * is_end(slots)).astype(BF16)
        for a in range(3):
            r = j - 2 + a
            if 0 <= r < slots:
                cat[r * cols:(r + 1) * cols, a * chan:(a + 1) * chan] = flat
    three(cat, wt, (2, 1, 0))

    @pl.loop(0, slots)
    def _(r):
        rows = y1[span(r), :] + later(y0[span(r), :]) + earlier(y2[span(r), :])
        ig_ref[r] = (rows * is_live(r)).astype(BF16)

    own = None
    for k in order:
        fd = lax.rem(f + k, shards)
        summed = dwbuf[fd, ch, c].astype(F32) + sbuf[k, ch].astype(F32)
        for j in range(1, chips):
            block = qbuf.at[k, j - 1]
            copy(block, block, q_s.at[k, j - 1], q_r.at[k, j - 1], t, f).wait_recv()
            summed = summed + qbuf[k, j - 1].astype(F32)
        if k == 0:
            own = summed
        else:
            zbuf[k - 1] = summed.astype(BF16)
            push(zbuf.at[k - 1], rbuf.at[k - 1], r_s.at[k - 1], r_r.at[k - 1], t, fd)
    for k in range(1, shards):
        block = rbuf.at[k - 1]
        copy(block, block, r_s.at[k - 1], r_r.at[k - 1], t, f).wait_recv()
        own = own + rbuf[k - 1].astype(F32)
    fbuf[t] = own.astype(BF16)
    mine = fbuf.at[t]
    for j in range(1, chips):
        push(mine, mine, f_s.at[j - 1], f_r.at[j - 1], peer_chip(j) * 2 + c, f)
    push(mine, mine, e_s.at[0], e_r.at[0], sibling, f)

    scale = float(shards * ROWS_MEAN * tiles * cols) ** (-0.5)
    for k in range(1, shards):
        block = sz.at[lax.rem(f + shards - k, shards)]
        copy(block, block, sz_s.at[k - 1], sz_r.at[k - 1], t, f).wait_recv()
    every = sz[0]
    for i in range(1, shards):
        every = every + sz[i]
    gg_ref[...] = every[0:1] * scale
    bg_ref[...] = every[1:2] * scale

    for j in range(1, chips):
        block = fbuf.at[from_chip(j) * 2 + c]
        copy(block, block, f_s.at[j - 1], f_r.at[j - 1], t, f).wait_recv()
        push(block, block, e_s.at[j], e_r.at[j], sibling, f)
    for j in range(chips):
        block = fbuf.at[from_chip(j) * 2 + (1 - c)]
        copy(block, block, e_s.at[j], e_r.at[j], sibling, f).wait_recv()

    for p in range(-(-shard // part)):
        low, high = p * part, min(shard, (p + 1) * part)
        at = slice(low, high)
        grad = fbuf[p].astype(F32)[:high - low] * scale
        wg_ref[at, :] = grad
        first = 0.9 * m1_ref[at, :] + 0.1 * grad
        second = 0.999 * m2_ref[at, :] + 0.001 * grad * grad
        n1_ref[at, :] = first
        n2_ref[at, :] = second
        first_fix = first / (1.0 - 0.9**10)
        second_fix = second / (1.0 - 0.999**10)
        nw_ref[at, :] = w_ref[at, :] - 0.01 * first_fix / (jnp.sqrt(second_fix) + 1e-08)

    for made in sent:
        made.wait_send()


def local(
    images, tile_rows, cotangent, master_weight, norm_gain, norm_bias, first_moment, second_moment
):
    slots, cols, chan = images.shape[2:]
    cells = slots * cols
    shard = master_weight.shape[0]
    tiles = lax.axis_size("tile")
    shards = lax.axis_size("fsdp")
    chips = tiles // 2
    part = -(-shard // (tiles * 16)) * 16
    group = jnp.arange(chan) // (chan // GROUPS)
    same = (group[:, None] == group[None, :]).astype(F32)
    vmem = pl.BlockSpec(memory_space=pltpu.VMEM)
    dma = pltpu.SemaphoreType.DMA
    aligned = shard % 16 == 0
    rows_out = jax.ShapeDtypeStruct((shard, chan), F32)
    pair = [dma((2,))] * 2
    picture = jax.ShapeDtypeStruct((slots, cols, chan), BF16)
    line = jax.ShapeDtypeStruct((1, chan), F32)
    flops = 3 * 2 * cells * 9 * chan * chan
    result = pl.pallas_call(
        functools.partial(kernel, tiles, shards, part),
        out_shape=(picture, picture, rows_out, rows_out, rows_out, rows_out, line, line),
        in_specs=[pl.BlockSpec(memory_space=pltpu.SMEM)] + [vmem] * 8,
        out_specs=(vmem,) * 8,
        scratch_shapes=[
            pltpu.VMEM((shards, tiles, part, chan), BF16),
            pltpu.VMEM((3, 3 * chan, chan), BF16),
            pltpu.VMEM((3, 3 * chan, chan), BF16),
            pltpu.VMEM((3 * chan, chan), F32),
            pltpu.VMEM((cells, 3 * chan), BF16),
            pltpu.VMEM((3 * chan, cells), BF16),
            pltpu.VMEM((cells, 3 * chan), BF16),
            pltpu.VMEM((cells, chan), F32),
            pltpu.VMEM((cells, chan), F32),
            pltpu.VMEM((cells, chan), F32),
            pltpu.VMEM((cells, chan), F32),
            pltpu.VMEM((cells, chan), BF16),
            pltpu.VMEM((slots, cols, chan), BF16),
            pltpu.VMEM((cells, chan), BF16),
            pltpu.VMEM((2, cols, chan), BF16),
            pltpu.VMEM((2, cols, chan), BF16),
            pltpu.VMEM((2, cols, chan), BF16),
            pltpu.VMEM((2, cols, chan), BF16),
            pltpu.VMEM((tiles, 8, chan), F32),
            pltpu.VMEM((tiles, 8, chan), F32),
            pltpu.VMEM((shards, 8, chan), F32),
            pltpu.VMEM((shards, chips, 2, part, chan), BF16),
            pltpu.VMEM((8 if aligned else shards * shard, chan), F32),
            pltpu.VMEM((shards, chips, part, chan), BF16),
            pltpu.VMEM((shards, chips - 1, part, chan), BF16),
            pltpu.VMEM((shards, chips - 1, part, chan), BF16),
            pltpu.VMEM((shards - 1, part, chan), BF16),
            pltpu.VMEM((shards - 1, part, chan), BF16),
            pltpu.VMEM((tiles, part, chan), BF16),
            dma((shards - 1,)), dma((shards - 1,)),
            dma((shards - 1, chips - 1)), dma((shards - 1, chips - 1)),
            dma((shards - 1, chips)), dma((shards - 1, chips)),
            *pair, *pair,
            dma((tiles - 1,)), dma((tiles - 1,)),
            dma((tiles - 1,)), dma((tiles - 1,)),
            dma((shards - 1,)), dma((shards - 1,)),
            dma((shards,)), dma((shards,)),
            dma((shards, chips - 1)), dma((shards, chips - 1)),
            dma((shards - 1,)), dma((shards - 1,)),
            dma((chips - 1,)), dma((chips - 1,)),
            dma((chips,)), dma((chips,)),
        ],
        compiler_params=pltpu.CompilerParams(
            collective_id=0, has_side_effects=True, vmem_limit_bytes=58 * 2**20
        ),
        cost_estimate=pl.CostEstimate(
            flops=flops, bytes_accessed=16 * 2**20, transcendentals=cells * chan
        ),
        name="conv_block",
    )(
        tile_rows, images[0, 0], cotangent[0, 0], master_weight,
        norm_gain[None], norm_bias[None], first_moment, second_moment, same,
    )
    act, ig, wg, nw, n1, n2, gg, bg = result
    return (act.reshape(images.shape), ig.reshape(images.shape), wg, nw, n1, n2, gg[0], bg[0])


def solution(mesh):
    tiled = P("fsdp", "tile", None, None, None)
    rows = P("fsdp", None)
    return jax.shard_map(
        local,
        mesh=mesh,
        in_specs=(tiled, P("fsdp", "tile"), tiled, rows, P(), P(), rows, rows),
        out_specs=(tiled, tiled, rows, rows, rows, rows, P(), P()),
        check_vma=False,
    )
```

time: 265 us -> 92.6 us (0.35)
  blocking collectives: 78.1 us -> 0 us
  Pallas kernels: 0 us -> 70.1 us
  waiting for transfers between devices: 68.7 us -> 0 us
  local copies, waits for them, and re-layouts: 61.8 us -> 18.8 us
  matrix products: 15.6 us -> 0 us
  between operations: 14.7 us -> 1.41 us
  starting transfers between devices: 11.5 us -> 0 us
  other arithmetic: 12.8 us -> 2.09 us
    psum x4 -> x0, blocking collectives: 78.1 us -> none  [the longest x1 40.6 us: local(): lax.psum((jnp.sum(dshift * normed, axis=0), jnp.sum(dshift, axis=0)), ('t...]
    pallas_call x0 -> x1, Pallas kernels: none -> 70.1 us  [local(): pl.pallas_call(functools.partial(kernel, tiles, shards, part), out_shape=...]
    psum x1 -> x0, waiting for transfers between devices: 49.4 us -> none  [local(): lax.psum(lax.dot_general(columns, pre_grad, (((0,), (0,)), ((), ())), pre...]
    concatenate x5 -> x0, local copies, waits for them, and re-layouts: 19.3 us -> none  [the longest x4 19.2 us: patches_of(): return jnp.concatenate(pieces, axis=-1).reshape(slot_count * cell_cols, -1)]
    all_gather x1 -> x0, waiting for transfers between devices: 19.3 us -> none  [local(): lax.all_gather(master_weight.astype(jnp.bfloat16), 'fsdp', axis=0, tiled=...]
    dot_general x3 -> x0, matrix products: 15.6 us -> none  [the longest x1 5.61 us: local(): mixed = jnp.dot(columns, gathered, preferred_element_type=jnp.float32)]
    ppermute x4 -> x0, starting transfers between devices: 11.3 us -> none  [the longest x2 6.37 us: extended(): lax.ppermute(tail, axis, [(i, (i + 1) % count) for i in range(ends)])]
    unnamed x41 -> x33, local copies, waits for them, and re-layouts: 26.3 us -> 16.3 us
  transfers between devices with their start and end apart: 7 -> 0, of which waited for: 2 -> 0; matrix products, arithmetic and copies ran while one was open for 22% -> 0% of each run, Pallas kernels for 0% -> 0%
where the time goes in v1:
time: 92.6 us; the launch traced here: 92.4 us
  Pallas kernels  70.1 us (76%)
  local copies, waits for them, and re-layouts  18.8 us (20%)
  other arithmetic  2.09 us (2%)
  between operations  1.41 us (2%)
    pallas_call x1, Pallas kernels, local(): pl.pallas_call(functools.partial(kernel, tiles, shards, part), out_shape=...  70.1 us
    unnamed x33, local copies, waits for them, and re-layouts  16.3 us

profile of v1, /device:TPU:1, one launch (start us, length us, event | category | flops | bytes accessed | tf_op | source)
XLA Modules:
  0.0 92.4 jit_solution(8461211091353548188)
XLA Ops:
  0.6 0.0 copy-start.8
  1.4 1.2 %broadcast_in_dim.8.gain_ref = f32[1,320]{1,0:T(1,128)} reshape(f32[320]{0:T(512)} %param.12) | data formatting | bytes 2560 | tf_op jit(solution)/shard_map/broadcast_in_dim | solution.py:498
  2.6 1.2 %broadcast_in_dim.9.bias_ref = f32[1,320]{1,0:T(1,128)} reshape(f32[320]{0:T(512)} %param.13) | data formatting | bytes 2560 | tf_op jit(solution)/shard_map/broadcast_in_dim | solution.py:498
  3.9 0.9 compare_convert_fusion.same_ref
  4.7 0.0 copy-start.4
  4.8 2.3 %copy.16 = bf16[1,1,8,128,320]{4,3,2,1,0:T(8,128)(2,1)} copy(bf16[1,1,8,128,320]{3,4,2,1,0:T(8,128)(2,1)} %param.8) | data formatting | bytes 1310720 | tf_op args[0]
  7.1 0.0 copy-done.8
  7.1 1.2 %copy.17 = bf16[1,1,8,128,320]{4,3,2,1,0:T(8,128)(2,1)} copy(bf16[1,1,8,128,320]{3,4,2,1,0:T(8,128)(2,1)S(1)} %copy-done.8) | data formatting | bytes 1310720 | tf_op args[2]
  8.2 0.0 copy-start.5
  8.2 0.0 copy-done.4
  8.2 1.3 %copy.18.w_ref = f32[720,320]{1,0:T(8,128)} copy(f32[720,320]{0,1:T(8,128)S(1)} %copy-done.4) | data formatting | bytes 1843200 | tf_op args[3]
  9.6 0.0 copy-done.5
  9.6 0.0 copy-start.6
  9.6 1.4 %copy.19.m1_ref = f32[720,320]{1,0:T(8,128)} copy(f32[720,320]{0,1:T(8,128)S(1)} %copy-done.5) | data formatting | bytes 1843200 | tf_op args[6]
  11.0 0.0 copy-done.6
  11.0 1.3 %copy.20.m2_ref = f32[720,320]{1,0:T(8,128)} copy(f32[720,320]{0,1:T(8,128)S(1)} %copy-done.6) | data formatting | bytes 1843200 | tf_op args[7]
  12.3 70.1 %conv_block.1 = (bf16[8,128,320]{2,1,0:T(8,128)(2,1)}, bf16[8,128,320]{2,1,0:T(8,128)(2,1)}, f32[720,320]{1,0:T(8,128)}, f32[720,320]{1,0:T(8,128)}, f32[720,320...) custom-call(s32[1,1]{1,0:T(1,128)S(6)} %copy.27.rows_ref, bf16[8,128,320]{2,1,0:T(8,128)(2,1)} %bitcast.6, ...), custom_call_target="tpu_custom_call" | custom-call | flops 5662310400 | bytes 16777216 | tf_op jit(solution)/shard_map/conv_block/pallas_call | solution.py:441
  82.4 0.0 copy-start.7
  82.4 0.0 copy-start.10
  82.4 0.0 copy-start.9
  82.5 0.0 copy-start.3
  82.5 2.4 %copy.21 = bf16[1,1,8,128,320]{3,4,2,1,0:T(8,128)(2,1)} copy(bf16[1,1,8,128,320]{4,3,2,1,0:T(8,128)(2,1)} %bitcast.5) | data formatting | bytes 1310720
  84.8 0.0 copy-done.7
  84.8 1.1 %copy.22 = bf16[1,1,8,128,320]{3,4,2,1,0:T(8,128)(2,1)} copy(bf16[1,1,8,128,320]{4,3,2,1,0:T(8,128)(2,1)S(1)} %bitcast.4) | data formatting | bytes 1310720
  86.0 0.0 copy-done.10
  86.0 0.0 copy-start.2
  86.0 0.6 reduce
  86.6 0.0 copy-done.9
  86.6 0.6 reduce.1
  87.2 0.0 copy-done.3
  87.2 1.3 %copy.23 = f32[720,320]{0,1:T(8,128)} copy(f32[720,320]{1,0:T(8,128)S(1)} %copy-done.3) | data formatting | bytes 1843200
  88.5 0.0 copy-done.2
  88.5 0.0 copy-start.1
  88.5 1.3 %copy.24 = f32[720,320]{0,1:T(8,128)} copy(f32[720,320]{1,0:T(8,128)S(1)} %copy-done.2) | data formatting | bytes 1843200
  89.8 0.0 copy-done.1
  89.8 0.0 copy-start
  89.8 1.3 %copy.25 = f32[720,320]{0,1:T(8,128)} copy(f32[720,320]{1,0:T(8,128)S(1)} %copy-done.1) | data formatting | bytes 1843200
  91.1 0.0 copy-done
  91.1 1.3 %copy.26 = f32[720,320]{0,1:T(8,128)} copy(f32[720,320]{1,0:T(8,128)S(1)} %copy-done) | data formatting | bytes 1843200
  (1 shorter events, 0.0 us)
Async XLA Ops:
  0.6 6.4 %copy-start.8 = (bf16[1,1,8,128,320]{3,4,2,1,0:T(8,128)(2,1)S(1)}, bf16[1,1,8,128,320]{3,4,2,1,0:T(8,128)(2,1)}, u32[]{:S(2)}) copy-start(bf16[1,1,8,128,320]{3,4,2,1,0:T(8,128)(2,1)} %param.10) | copy-start | bytes 1966084
  4.7 3.5 %copy-start.4 = (f32[720,320]{0,1:T(8,128)S(1)}, f32[720,320]{0,1:T(8,128)}, u32[]{:S(2)}) copy-start(f32[720,320]{0,1:T(8,128)} %param.11) | copy-start | bytes 2764804
  8.2 1.4 %copy-start.5 = (f32[720,320]{0,1:T(8,128)S(1)}, f32[720,320]{0,1:T(8,128)}, u32[]{:S(2)}) copy-start(f32[720,320]{0,1:T(8,128)} %param.14) | copy-start | bytes 2764804
  9.6 1.4 %copy-start.6 = (f32[720,320]{0,1:T(8,128)S(1)}, f32[720,320]{0,1:T(8,128)}, u32[]{:S(2)}) copy-start(f32[720,320]{0,1:T(8,128)} %param.15) | copy-start | bytes 2764804
  82.4 2.4 %copy-start.7 = (bf16[8,128,320]{2,1,0:T(8,128)(2,1)S(1)}, bf16[8,128,320]{2,1,0:T(8,128)(2,1)}, u32[]{:S(2)}) copy-start(bf16[8,128,320]{2,1,0:T(8,128)(2,1)} %get-tuple-element.17) | copy-start | bytes 1966084
  82.4 3.5 %copy-start.10 = (f32[1,320]{1,0:T(1,128)S(1)}, f32[1,320]{1,0:T(1,128)}, u32[]{:S(2)}) copy-start(f32[1,320]{1,0:T(1,128)} %get-tuple-element.22) | copy-start | bytes 3844
  82.4 4.1 %copy-start.9 = (f32[1,320]{1,0:T(1,128)S(1)}, f32[1,320]{1,0:T(1,128)}, u32[]{:S(2)}) copy-start(f32[1,320]{1,0:T(1,128)} %get-tuple-element.23) | copy-start | bytes 3844
  82.5 4.7 %copy-start.3 = (f32[720,320]{1,0:T(8,128)S(1)}, f32[720,320]{1,0:T(8,128)}, u32[]{:S(2)}) copy-start(f32[720,320]{1,0:T(8,128)} %get-tuple-element.26) | copy-start | bytes 2764804
  86.0 2.5 %copy-start.2 = (f32[720,320]{1,0:T(8,128)S(1)}, f32[720,320]{1,0:T(8,128)}, u32[]{:S(2)}) copy-start(f32[720,320]{1,0:T(8,128)} %get-tuple-element.27) | copy-start | bytes 2764804
  88.5 1.3 %copy-start.1 = (f32[720,320]{1,0:T(8,128)S(1)}, f32[720,320]{1,0:T(8,128)}, u32[]{:S(2)}) copy-start(f32[720,320]{1,0:T(8,128)} %get-tuple-element.28) | copy-start | bytes 2764804
  89.8 1.3 %copy-start = (f32[720,320]{1,0:T(8,128)S(1)}, f32[720,320]{1,0:T(8,128)}, u32[]{:S(2)}) copy-start(f32[720,320]{1,0:T(8,128)} %get-tuple-element.29) | copy-start | bytes 2764804

commit v2 on v1

--- a/solution.py
+++ b/solution.py
@@ -29,17 +29,18 @@
 
 def kernel(
     tiles, shards, part,
-    rows_ref, x_ref, ct_ref, w_ref, gain_ref, bias_ref, m1_ref, m2_ref, same_ref,
-    act_ref, ig_ref, wg_ref, nw_ref, n1_ref, n2_ref, gg_ref, bg_ref,
+    rows_ref, x_ref, ct_any, w_ref, gain_ref, bias_ref, m1_any, m2_any,
+    act_any, ig_any, wg_ref, nw_ref, n1_ref, n2_ref, gg_ref, bg_ref,
+    ct_ref, m1_ref, m2_ref, act_ref, ig_ref, same_ref, wrow, loc,
     gath, wb, wt, wide, xcat, xcat_t, cat, y0, y1, y2, up, g0, g1, g2,
     hs, hr, hs2, hr2, st, sd, sz,
     dwbuf, dwf, sbuf, pbuf, qbuf, zbuf, rbuf, fbuf,
     z_s, z_r, p_s, p_r, s_s, s_r, h_s, h_r, h2_s, h2_r, st_s, st_r, sd_s, sd_r, sz_s, sz_r,
     b_s, b_r, q_s, q_r, r_s, r_r, f_s, f_r, e_s, e_r,
 ):
-    slots, cols, chan = x_ref.shape
+    slots, chan, cols = x_ref.shape
     cells = slots * cols
-    shard = w_ref.shape[0]
+    shard = w_ref.shape[1]
     total = shards * shard
     chips = tiles // 2
     t = lax.axis_index("tile")
@@ -73,12 +74,20 @@
     for k in range(1, shards):
         pl.semaphore_signal(barrier, inc=1, device_id=(t, lax.rem(f + k, shards)), device_id_type=MESH)
 
+    loads = [
+        pltpu.make_async_copy(src, dst, loc.at[i])
+        for i, (src, dst) in enumerate(((ct_any, ct_ref), (m1_any, m1_ref), (m2_any, m2_ref)))
+    ]
+    for load in loads:
+        load.start()
+
+    wrow[...] = w_ref[...].T
     for p in range(tiles):
         low, high = p * part, min(shard, (p + 1) * part)
         if high <= low:
             gath[f, p] = jnp.zeros((part, chan), BF16)
         else:
-            rows = w_ref[low:high, :]
+            rows = wrow[low:high, :]
             if high - low < part:
                 rows = jnp.concatenate([rows, jnp.zeros((part - high + low, chan), F32)], axis=0)
             gath[f, p] = rows.astype(BF16)
@@ -103,7 +112,7 @@
 
         @pl.when(t == 0)
         def _():
-            dst[0] = jnp.zeros((cols, chan), BF16)
+            dst[0] = jnp.zeros(dst.shape[1:], BF16)
 
         @pl.when(t < tiles - 1)
         def _():
@@ -111,7 +120,7 @@
 
         @pl.when(t == tiles - 1)
         def _():
-            dst[1] = jnp.zeros((cols, chan), BF16)
+            dst[1] = jnp.zeros(dst.shape[1:], BF16)
 
     def halo_wait(src, dst, send, recv):
         up_copy, down_copy = halo_copies(src, dst, send, recv)
@@ -152,12 +161,20 @@
             value = x_ref[j - 1].astype(F32) * is_live(j - 1) + below * is_end(j - 1)
         else:
             value = below * is_end(slots)
-        flat, turned = value.astype(BF16), value.T.astype(BF16)
+        flat, turned = value.T.astype(BF16), value.astype(BF16)
         for a in range(3):
             r = j - a
             if 0 <= r < slots:
                 xcat[r * cols:(r + 1) * cols, a * chan:(a + 1) * chan] = flat
                 xcat_t[a * chan:(a + 1) * chan, r * cols:(r + 1) * cols] = turned
+
+    loads[0].wait()
+    for r in range(slots):
+        up[r * cols:(r + 1) * cols, :] = ct_ref[r].astype(F32).T
+    across = lax.broadcasted_iota(jnp.int32, (chan, chan), 1).astype(F32)
+    down = lax.broadcasted_iota(jnp.int32, (chan, chan), 0).astype(F32)
+    per = float(chan // GROUPS)
+    same_ref[...] = (jnp.floor((across + 0.5) / per) == jnp.floor((down + 0.5) / per)).astype(F32)
 
     for k in range(1, shards):
         fs = lax.rem(f + shards - k, shards)
@@ -259,7 +276,7 @@
         apart = st[i, 0:1, :] - mean
         spread = spread + st[i, 1:2, :] + st[i, 2:3, :] * apart * apart
     inverse = lax.rsqrt(spread / population + 1e-05)
-    gain, bias = gain_ref[...], bias_ref[...]
+    gain, bias = gain_ref[...].reshape(1, chan), bias_ref[...].reshape(1, chan)
 
     def gate(r, sums):
         gains, biases = sums
@@ -267,8 +284,8 @@
         normed = (y1[span(r), :] - mean) * inverse
         shifted = normed * gain + bias
         s = jax.nn.sigmoid(shifted)
-        act_ref[r] = (shifted * s * mask).astype(BF16)
-        dshift = ct_ref[r].astype(F32) * mask * s * (1.0 + shifted * (1.0 - s))
+        act_ref[r] = (shifted * s * mask).T.astype(BF16)
+        dshift = up[span(r), :] * mask * s * (1.0 + shifted * (1.0 - s))
         y1[span(r), :] = normed
         up[span(r), :] = dshift
         return (
@@ -277,6 +294,8 @@
         )
 
     own_gain, own_bias = lax.fori_loop(0, slots, gate, (zero_row, zero_row))
+    act_out = pltpu.make_async_copy(act_ref, act_any, loc.at[3])
+    act_out.start()
     sd[t] = jnp.concatenate([own_gain, own_bias, jnp.zeros((6, chan), F32)], axis=0)
     tile_share(sd, sd_s, sd_r)
     tile_wait(sd, sd_s, sd_r)
@@ -358,7 +377,10 @@
     @pl.loop(0, slots)
     def _(r):
         rows = y1[span(r), :] + later(y0[span(r), :]) + earlier(y2[span(r), :])
-        ig_ref[r] = (rows * is_live(r)).astype(BF16)
+        ig_ref[r] = (rows * is_live(r)).T.astype(BF16)
+
+    ig_out = pltpu.make_async_copy(ig_ref, ig_any, loc.at[4])
+    ig_out.start()
 
     own = None
     for k in order:
@@ -390,8 +412,8 @@
     every = sz[0]
     for i in range(1, shards):
         every = every + sz[i]
-    gg_ref[...] = every[0:1] * scale
-    bg_ref[...] = every[1:2] * scale
+    gg_ref[...] = (every[0:1] * scale).reshape(chan)
+    bg_ref[...] = (every[1:2] * scale).reshape(chan)
 
     for j in range(1, chips):
         block = fbuf.at[from_chip(j) * 2 + c]
@@ -403,19 +425,27 @@
 
     for p in range(-(-shard // part)):
         low, high = p * part, min(shard, (p + 1) * part)
-        at = slice(low, high)
-        grad = fbuf[p].astype(F32)[:high - low] * scale
-        wg_ref[at, :] = grad
-        first = 0.9 * m1_ref[at, :] + 0.1 * grad
-        second = 0.999 * m2_ref[at, :] + 0.001 * grad * grad
-        n1_ref[at, :] = first
-        n2_ref[at, :] = second
-        first_fix = first / (1.0 - 0.9**10)
-        second_fix = second / (1.0 - 0.999**10)
-        nw_ref[at, :] = w_ref[at, :] - 0.01 * first_fix / (jnp.sqrt(second_fix) + 1e-08)
-
+        wrow[low:high, :] = fbuf[p].astype(F32)[:high - low]
+    loads[1].wait()
+    loads[2].wait()
+    grad = wrow[...].T * scale
+    wg_ref[...] = grad
+    first = 0.9 * m1_ref[...] + 0.1 * grad
+    second = 0.999 * m2_ref[...] + 0.001 * grad * grad
+    n1_ref[...] = first
+    n2_ref[...] = second
+    first_fix = first / (1.0 - 0.9**10)
+    second_fix = second / (1.0 - 0.999**10)
+    nw_ref[...] = w_ref[...] - 0.01 * first_fix / (jnp.sqrt(second_fix) + 1e-08)
+
+    act_out.wait()
+    ig_out.wait()
     for made in sent:
         made.wait_send()
+
+
+def swapped(array):
+    return jnp.swapaxes(array, 1, 2)
 
 
 def local(
@@ -428,22 +458,31 @@
     shards = lax.axis_size("fsdp")
     chips = tiles // 2
     part = -(-shard // (tiles * 16)) * 16
-    group = jnp.arange(chan) // (chan // GROUPS)
-    same = (group[:, None] == group[None, :]).astype(F32)
+    anywhere = pl.BlockSpec(memory_space=pl.ANY)
     vmem = pl.BlockSpec(memory_space=pltpu.VMEM)
     dma = pltpu.SemaphoreType.DMA
     aligned = shard % 16 == 0
-    rows_out = jax.ShapeDtypeStruct((shard, chan), F32)
+    rows_out = jax.ShapeDtypeStruct((chan, shard), F32)
     pair = [dma((2,))] * 2
-    picture = jax.ShapeDtypeStruct((slots, cols, chan), BF16)
-    line = jax.ShapeDtypeStruct((1, chan), F32)
+    picture = jax.ShapeDtypeStruct((slots, chan, cols), BF16)
+    line = jax.ShapeDtypeStruct((chan,), F32)
     flops = 3 * 2 * cells * 9 * chan * chan
     result = pl.pallas_call(
         functools.partial(kernel, tiles, shards, part),
         out_shape=(picture, picture, rows_out, rows_out, rows_out, rows_out, line, line),
-        in_specs=[pl.BlockSpec(memory_space=pltpu.SMEM)] + [vmem] * 8,
-        out_specs=(vmem,) * 8,
+        in_specs=[
+            pl.BlockSpec(memory_space=pltpu.SMEM), vmem, anywhere, vmem, vmem, vmem, anywhere, anywhere
+        ],
+        out_specs=(anywhere, anywhere) + (vmem,) * 6,
         scratch_shapes=[
+            pltpu.VMEM((slots, chan, cols), BF16),
+            pltpu.VMEM((chan, shard), F32),
+            pltpu.VMEM((chan, shard), F32),
+            pltpu.VMEM((slots, chan, cols), BF16),
+            pltpu.VMEM((slots, chan, cols), BF16),
+            pltpu.VMEM((chan, chan), F32),
+            pltpu.VMEM((shard, chan), F32),
+            dma((5,)),
             pltpu.VMEM((shards, tiles, part, chan), BF16),
             pltpu.VMEM((3, 3 * chan, chan), BF16),
             pltpu.VMEM((3, 3 * chan, chan), BF16),
@@ -458,8 +497,8 @@
             pltpu.VMEM((cells, chan), BF16),
             pltpu.VMEM((slots, cols, chan), BF16),
             pltpu.VMEM((cells, chan), BF16),
-            pltpu.VMEM((2, cols, chan), BF16),
-            pltpu.VMEM((2, cols, chan), BF16),
+            pltpu.VMEM((2, chan, cols), BF16),
+            pltpu.VMEM((2, chan, cols), BF16),
             pltpu.VMEM((2, cols, chan), BF16),
             pltpu.VMEM((2, cols, chan), BF16),
             pltpu.VMEM((tiles, 8, chan), F32),
@@ -494,11 +533,12 @@
         ),
         name="conv_block",
     )(
-        tile_rows, images[0, 0], cotangent[0, 0], master_weight,
-        norm_gain[None], norm_bias[None], first_moment, second_moment, same,
+        tile_rows, swapped(images[0, 0]), swapped(cotangent[0, 0]), master_weight.T,
+        norm_gain, norm_bias, first_moment.T, second_moment.T,
     )
     act, ig, wg, nw, n1, n2, gg, bg = result
-    return (act.reshape(images.shape), ig.reshape(images.shape), wg, nw, n1, n2, gg[0], bg[0])
+    act, ig = swapped(act).reshape(images.shape), swapped(ig).reshape(images.shape)
+    return (act, ig, wg.T, nw.T, n1.T, n2.T, gg, bg)
 
 
 def solution(mesh):

time: 92.6 us -> 80.4 us (0.87)
  local copies, waits for them, and re-layouts: 18.8 us -> 10.4 us
  other arithmetic: 2.09 us -> 0 us
  Pallas kernels: 70.1 us -> 68.4 us
    unnamed x33 -> x22, local copies, waits for them, and re-layouts: 16.3 us -> 10.4 us
    broadcast_in_dim x2 -> x0, local copies, waits for them, and re-layouts: 2.49 us -> none  [the longest x1 1.25 us: local(): norm_gain[None]]
    pallas_call x1, Pallas kernels: 70.1 us -> 68.4 us  [local(): pl.pallas_call(functools.partial(kernel, tiles, shards, part), out_shape=...]
    pallas_call x2 -> x0, other arithmetic: 1.19 us -> none  [local(): pl.pallas_call(functools.partial(kernel, tiles, shards, part), out_shape=...]
where the time goes in v2:
time: 80.4 us; the launch traced here: 80 us
  Pallas kernels  68.4 us (85%)
  local copies, waits for them, and re-layouts  10.4 us (13%)
  between operations  1.31 us (2%)
    pallas_call x1, Pallas kernels, local(): pl.pallas_call(functools.partial(kernel, tiles, shards, part), out_shape=...  68.4 us
    unnamed x22, local copies, waits for them, and re-layouts  10.4 us

profile of v2, /device:TPU:1, one launch (start us, length us, event | category | flops | bytes accessed | tf_op | source)
XLA Modules:
  0.0 80.0 jit_solution(10002433943240048137)
XLA Ops:
  1.3 68.4 %conv_block.1 = (bf16[8,320,128]{2,1,0:T(8,128)(2,1)}, bf16[8,320,128]{2,1,0:T(8,128)(2,1)}, f32[320,720]{1,0:T(8,128)}, f32[320,720]{1,0:T(8,128)}, f32[320,720...) custom-call(s32[1,1]{1,0:T(1,128)S(6)} %copy.24.rows_ref, bf16[8,320,128]{2,1,0:T(8,128)(2,1)} %bitcast.28, ...), custom_call_target="tpu_custom_call" | custom-call | flops 5662310400 | bytes 16777216 | tf_op jit(solution)/shard_map/conv_block/pallas_call | solution.py:470
  69.7 0.0 copy-start.4
  69.7 2.0 %copy.25 = bf16[1,1,8,128,320]{3,4,2,1,0:T(8,128)(2,1)} copy(bf16[1,1,8,128,320]{3,4,2,1,0:T(8,128)(2,1)} %bitcast.24) | data formatting | bytes 1310720
  71.7 0.0 copy-done.4
  71.7 0.0 copy-start.3
  71.7 0.8 %copy.26 = bf16[1,1,8,128,320]{3,4,2,1,0:T(8,128)(2,1)} copy(bf16[1,1,8,128,320]{3,4,2,1,0:T(8,128)(2,1)S(1)} %bitcast.23) | data formatting | bytes 1310720
  72.5 0.6 copy-done.3
  73.1 0.0 copy-start.2
  73.1 0.9 %copy.27 = f32[720,320]{0,1:T(8,128)} copy(f32[720,320]{0,1:T(8,128)S(1)} %bitcast.22) | data formatting | bytes 1843200
  74.1 0.6 copy-done.2
  74.7 0.0 copy-start.1
  74.7 0.9 %copy.28 = f32[720,320]{0,1:T(8,128)} copy(f32[720,320]{0,1:T(8,128)S(1)} %bitcast.21) | data formatting | bytes 1843200
  75.6 0.6 copy-done.1
  76.3 0.0 copy-start
  76.3 0.9 %copy.29 = f32[720,320]{0,1:T(8,128)} copy(f32[720,320]{0,1:T(8,128)S(1)} %bitcast.20) | data formatting | bytes 1843200
  77.2 0.6 copy-done
  77.8 0.0 copy-start.6
  77.8 0.9 %copy.30 = f32[720,320]{0,1:T(8,128)} copy(f32[720,320]{0,1:T(8,128)S(1)} %bitcast.19) | data formatting | bytes 1843200
  78.8 0.0 copy-done.6
  78.8 0.0 copy-start.5
  78.8 0.6 copy.31
  79.3 0.1 copy-done.5
  79.4 0.6 copy.32
Async XLA Ops:
  69.7 2.0 %copy-start.4 = (bf16[8,320,128]{2,1,0:T(8,128)(2,1)S(1)}, bf16[8,320,128]{2,1,0:T(8,128)(2,1)}, u32[]{:S(2)}) copy-start(bf16[8,320,128]{2,1,0:T(8,128)(2,1)} %get-tuple-element.17) | copy-start | bytes 1966084
  71.7 1.4 %copy-start.3 = (f32[320,720]{1,0:T(8,128)S(1)}, f32[320,720]{1,0:T(8,128)}, u32[]{:S(2)}) copy-start(f32[320,720]{1,0:T(8,128)} %get-tuple-element.18) | copy-start | bytes 2764804
  73.1 1.6 %copy-start.2 = (f32[320,720]{1,0:T(8,128)S(1)}, f32[320,720]{1,0:T(8,128)}, u32[]{:S(2)}) copy-start(f32[320,720]{1,0:T(8,128)} %get-tuple-element.19) | copy-start | bytes 2764804
  74.7 1.6 %copy-start.1 = (f32[320,720]{1,0:T(8,128)S(1)}, f32[320,720]{1,0:T(8,128)}, u32[]{:S(2)}) copy-start(f32[320,720]{1,0:T(8,128)} %get-tuple-element.20) | copy-start | bytes 2764804
  76.3 1.6 %copy-start = (f32[320,720]{1,0:T(8,128)S(1)}, f32[320,720]{1,0:T(8,128)}, u32[]{:S(2)}) copy-start(f32[320,720]{1,0:T(8,128)} %get-tuple-element.21) | copy-start | bytes 2764804
  77.8 0.9 %copy-start.6 = (f32[320]{0:T(512)S(1)}, f32[320]{0:T(512)}, u32[]{:S(2)}) copy-start(f32[320]{0:T(512)} %get-tuple-element.38) | copy-start | bytes 3844
  78.8 0.7 copy-start.5

commit v3 on v2

--- a/solution.py
+++ b/solution.py
@@ -29,9 +29,9 @@
 
 def kernel(
     tiles, shards, part,
-    rows_ref, x_ref, ct_any, w_ref, gain_ref, bias_ref, m1_any, m2_any,
-    act_any, ig_any, wg_ref, nw_ref, n1_ref, n2_ref, gg_ref, bg_ref,
-    ct_ref, m1_ref, m2_ref, act_ref, ig_ref, same_ref, wrow, loc,
+    rows_ref, x_ref, ct_any, w_ref, gain_ref, bias_ref,
+    act_any, ig_any, wg_ref, gg_ref, bg_ref,
+    ct_ref, act_ref, ig_ref, same_ref, wrow, loc,
     gath, wb, wt, wide, xcat, xcat_t, cat, y0, y1, y2, up, g0, g1, g2,
     hs, hr, hs2, hr2, st, sd, sz,
     dwbuf, dwf, sbuf, pbuf, qbuf, zbuf, rbuf, fbuf,
@@ -74,12 +74,8 @@
     for k in range(1, shards):
         pl.semaphore_signal(barrier, inc=1, device_id=(t, lax.rem(f + k, shards)), device_id_type=MESH)
 
-    loads = [
-        pltpu.make_async_copy(src, dst, loc.at[i])
-        for i, (src, dst) in enumerate(((ct_any, ct_ref), (m1_any, m1_ref), (m2_any, m2_ref)))
-    ]
-    for load in loads:
-        load.start()
+    ct_in = pltpu.make_async_copy(ct_any, ct_ref, loc.at[0])
+    ct_in.start()
 
     wrow[...] = w_ref[...].T
     for p in range(tiles):
@@ -168,7 +164,7 @@
                 xcat[r * cols:(r + 1) * cols, a * chan:(a + 1) * chan] = flat
                 xcat_t[a * chan:(a + 1) * chan, r * cols:(r + 1) * cols] = turned
 
-    loads[0].wait()
+    ct_in.wait()
     for r in range(slots):
         up[r * cols:(r + 1) * cols, :] = ct_ref[r].astype(F32).T
     across = lax.broadcasted_iota(jnp.int32, (chan, chan), 1).astype(F32)
@@ -294,7 +290,7 @@
         )
 
     own_gain, own_bias = lax.fori_loop(0, slots, gate, (zero_row, zero_row))
-    act_out = pltpu.make_async_copy(act_ref, act_any, loc.at[3])
+    act_out = pltpu.make_async_copy(act_ref, act_any, loc.at[1])
     act_out.start()
     sd[t] = jnp.concatenate([own_gain, own_bias, jnp.zeros((6, chan), F32)], axis=0)
     tile_share(sd, sd_s, sd_r)
@@ -305,8 +301,8 @@
     sz[f] = frame
     for k in range(1, shards):
         push(sz.at[f], sz.at[f], sz_s.at[k - 1], sz_r.at[k - 1], t, lax.rem(f + k, shards))
-    delta = group_sum(frame[1:2] * gain) / population
-    cross = group_sum(frame[0:1] * gain) / population
+    both = group_sum(frame * gain) / population
+    cross, delta = both[0:1], both[1:2]
 
     @pl.loop(0, slots)
     def _(r):
@@ -379,7 +375,7 @@
         rows = y1[span(r), :] + later(y0[span(r), :]) + earlier(y2[span(r), :])
         ig_ref[r] = (rows * is_live(r)).T.astype(BF16)
 
-    ig_out = pltpu.make_async_copy(ig_ref, ig_any, loc.at[4])
+    ig_out = pltpu.make_async_copy(ig_ref, ig_any, loc.at[2])
     ig_out.start()
 
     own = None
@@ -426,22 +422,31 @@
     for p in range(-(-shard // part)):
         low, high = p * part, min(shard, (p + 1) * part)
         wrow[low:high, :] = fbuf[p].astype(F32)[:high - low]
-    loads[1].wait()
-    loads[2].wait()
-    grad = wrow[...].T * scale
-    wg_ref[...] = grad
-    first = 0.9 * m1_ref[...] + 0.1 * grad
-    second = 0.999 * m2_ref[...] + 0.001 * grad * grad
-    n1_ref[...] = first
-    n2_ref[...] = second
-    first_fix = first / (1.0 - 0.9**10)
-    second_fix = second / (1.0 - 0.999**10)
-    nw_ref[...] = w_ref[...] - 0.01 * first_fix / (jnp.sqrt(second_fix) + 1e-08)
+    wg_ref[...] = wrow[...].T.astype(BF16)
 
     act_out.wait()
     ig_out.wait()
     for made in sent:
         made.wait_send()
+
+
+def adam(
+    scale, act_ref, ig_ref, grad_ref, w_ref, m1_ref, m2_ref, gg_ref, bg_ref,
+    act_out, ig_out, wg_out, nw_out, n1_out, n2_out, gg_out, bg_out,
+):
+    act_out[...] = act_ref[...]
+    ig_out[...] = ig_ref[...]
+    gg_out[...] = gg_ref[...]
+    bg_out[...] = bg_ref[...]
+    grad = grad_ref[...].astype(F32) * scale
+    wg_out[...] = grad
+    first = 0.9 * m1_ref[...] + 0.1 * grad
+    second = 0.999 * m2_ref[...] + 0.001 * grad * grad
+    n1_out[...] = first
+    n2_out[...] = second
+    first_fix = first / (1.0 - 0.9**10)
+    second_fix = second / (1.0 - 0.999**10)
+    nw_out[...] = w_ref[...] - 0.01 * first_fix / (jnp.sqrt(second_fix) + 1e-08)
 
 
 def swapped(array):
@@ -463,26 +468,25 @@
     dma = pltpu.SemaphoreType.DMA
     aligned = shard % 16 == 0
     rows_out = jax.ShapeDtypeStruct((chan, shard), F32)
+    grad_out = jax.ShapeDtypeStruct((chan, shard), BF16)
     pair = [dma((2,))] * 2
     picture = jax.ShapeDtypeStruct((slots, chan, cols), BF16)
     line = jax.ShapeDtypeStruct((chan,), F32)
     flops = 3 * 2 * cells * 9 * chan * chan
     result = pl.pallas_call(
         functools.partial(kernel, tiles, shards, part),
-        out_shape=(picture, picture, rows_out, rows_out, rows_out, rows_out, line, line),
+        out_shape=(picture, picture, grad_out, line, line),
         in_specs=[
-            pl.BlockSpec(memory_space=pltpu.SMEM), vmem, anywhere, vmem, vmem, vmem, anywhere, anywhere
+            pl.BlockSpec(memory_space=pltpu.SMEM), vmem, anywhere, vmem, vmem, vmem
         ],
-        out_specs=(anywhere, anywhere) + (vmem,) * 6,
+        out_specs=(anywhere, anywhere) + (vmem,) * 3,
         scratch_shapes=[
             pltpu.VMEM((slots, chan, cols), BF16),
-            pltpu.VMEM((chan, shard), F32),
-            pltpu.VMEM((chan, shard), F32),
             pltpu.VMEM((slots, chan, cols), BF16),
             pltpu.VMEM((slots, chan, cols), BF16),
             pltpu.VMEM((chan, chan), F32),
             pltpu.VMEM((shard, chan), F32),
-            dma((5,)),
+            dma((3,)),
             pltpu.VMEM((shards, tiles, part, chan), BF16),
             pltpu.VMEM((3, 3 * chan, chan), BF16),
             pltpu.VMEM((3, 3 * chan, chan), BF16),
@@ -534,9 +538,23 @@
         name="conv_block",
     )(
         tile_rows, swapped(images[0, 0]), swapped(cotangent[0, 0]), master_weight.T,
-        norm_gain, norm_bias, first_moment.T, second_moment.T,
+        norm_gain, norm_bias,
     )
-    act, ig, wg, nw, n1, n2, gg, bg = result
+    act, ig, wg, gg, bg = result
+    steps = 4
+    slab = pl.BlockSpec((slots // steps, chan, cols), lambda i: (i, 0, 0))
+    strip = pl.BlockSpec((chan // steps, shard), lambda i: (i, 0))
+    whole = pl.BlockSpec((chan,), lambda i: (0,))
+    scale = float(shards * ROWS_MEAN * tiles * cols) ** (-0.5)
+    act, ig, wg, nw, n1, n2, gg, bg = pl.pallas_call(
+        functools.partial(adam, scale),
+        grid=(steps,),
+        out_shape=(picture, picture, rows_out, rows_out, rows_out, rows_out, line, line),
+        in_specs=[slab, slab, strip, strip, strip, strip, whole, whole],
+        out_specs=(slab, slab, strip, strip, strip, strip, whole, whole),
+        compiler_params=pltpu.CompilerParams(vmem_limit_bytes=32 * 2**20),
+        name="adam_step",
+    )(act, ig, wg, master_weight.T, first_moment.T, second_moment.T, gg, bg)
     act, ig = swapped(act).reshape(images.shape), swapped(ig).reshape(images.shape)
     return (act, ig, wg.T, nw.T, n1.T, n2.T, gg, bg)
 

time: 80.4 us -> 75 us (0.933)
  local copies, waits for them, and re-layouts: 10.4 us -> 3.86 us
  Pallas kernels: 68.4 us -> 69.5 us
    unnamed x22 -> x16, local copies, waits for them, and re-layouts: 10.4 us -> 3.86 us
    pallas_call x0 -> x1, Pallas kernels: none -> 2.91 us  [local(): pl.pallas_call(functools.partial(adam, scale), grid=(steps,), out_shape=(...]
    pallas_call x1, Pallas kernels: 68.4 us -> 66.6 us  [local(): pl.pallas_call(functools.partial(kernel, tiles, shards, part), out_shape=...]
where the time goes in v3:
time: 75 us; the launch traced here: 74.7 us
  Pallas kernels  69.5 us (93%)
  local copies, waits for them, and re-layouts  3.86 us (5%)
  between operations  1.36 us (2%)
    pallas_call x1, Pallas kernels, local(): pl.pallas_call(functools.partial(kernel, tiles, shards, part), out_shape=...  66.6 us
    unnamed x16, local copies, waits for them, and re-layouts  3.86 us
    pallas_call x1, Pallas kernels, local(): pl.pallas_call(functools.partial(adam, scale), grid=(steps,), out_shape=(...  2.91 us

profile of v3, /device:TPU:1, one launch (start us, length us, event | category | flops | bytes accessed | tf_op | source)
XLA Modules:
  0.0 74.7 jit_solution(108083250060296092)
XLA Ops:
  1.3 0.0 copy-start
  1.3 0.0 copy-start.1
  1.3 0.0 copy-start.2
  1.3 66.6 %conv_block.1 = (bf16[8,320,128]{2,1,0:T(8,128)(2,1)}, bf16[8,320,128]{2,1,0:T(8,128)(2,1)}, bf16[320,720]{1,0:T(8,128)(2,1)}, f32[320]{0:T(512)}, f32[320]{0:T(512)}) custom-call(s32[1,1]{1,0:T(1,128)S(6)} %copy.16.rows_ref, bf16[8,320,128]{2,1,0:T(8,128)(2,1)} %bitcast.27, bf16[8,320,128]{2,1,0:T(8,128)(2,1)} %bitcast.28, f32[320,720]{1,0:T(8,128)} %bitcast.19, ...), custom_call_target="tpu_custom_call" | custom-call | flops 5662310400 | bytes 16777216 | tf_op jit(solution)/shard_map/conv_block/pallas_call | solution.py:476
  67.9 0.0 copy-start.7
  67.9 0.0 copy-start.6
  67.9 0.0 copy-done
  67.9 0.0 copy-done.1
  67.9 0.0 copy-done.2
  68.0 0.6 copy-done.7
  68.6 0.0 copy-done.6
  68.6 0.0 copy-start.3
  68.6 1.1 %copy-done.3 = bf16[8,320,128]{2,1,0:T(8,128)(2,1)S(1)} copy-done((bf16[8,320,128]{2,1,0:T(8,128)(2,1)S(1)}, bf16[8,320,128]{2,1,0:T(8,128)(2,1)}, u32[]{:S(2)}) %copy-start.3) | copy-done | bytes 655384
  69.7 0.0 copy-start.4
  69.7 1.1 %copy-done.4 = bf16[8,320,128]{2,1,0:T(8,128)(2,1)S(1)} copy-done((bf16[8,320,128]{2,1,0:T(8,128)(2,1)S(1)}, bf16[8,320,128]{2,1,0:T(8,128)(2,1)}, u32[]{:S(2)}) %copy-start.4) | copy-done | bytes 655384
  70.8 0.0 copy-start.5
  70.8 1.0 %copy-done.5 = bf16[320,720]{1,0:T(8,128)(2,1)S(1)} copy-done((bf16[320,720]{1,0:T(8,128)(2,1)S(1)}, bf16[320,720]{1,0:T(8,128)(2,1)}, u32[]{:S(2)}) %copy-start.5) | copy-done | bytes 460824
  71.8 2.9 %adam_step.1 = (bf16[8,320,128]{2,1,0:T(8,128)(2,1)}, bf16[8,320,128]{2,1,0:T(8,128)(2,1)}, f32[320,720]{1,0:T(8,128)}, f32[320,720]{1,0:T(8,128)}, f32[320,720]...) custom-call(bf16[8,320,128]{2,1,0:T(8,128)(2,1)S(1)} %copy-done.3, bf16[8,320,128]{2,1,0:T(8,128)(2,1)S(1)} %copy-done.4, ...), custom_call_target="tpu_custom_call" | custom-call | tf_op jit(solution)/shard_map/adam_step/pallas_call | solution.py:549
Async XLA Ops:
  1.3 66.6 %copy-start = (f32[720,320]{0,1:T(8,128)S(1)}, f32[720,320]{0,1:T(8,128)}, u32[]{:S(2)}) copy-start(f32[720,320]{0,1:T(8,128)} %param.11) | copy-start | bytes 2764804
  1.3 66.6 %copy-start.1 = (f32[720,320]{0,1:T(8,128)S(1)}, f32[720,320]{0,1:T(8,128)}, u32[]{:S(2)}) copy-start(f32[720,320]{0,1:T(8,128)} %param.14) | copy-start | bytes 2764804
  1.3 66.6 %copy-start.2 = (f32[720,320]{0,1:T(8,128)S(1)}, f32[720,320]{0,1:T(8,128)}, u32[]{:S(2)}) copy-start(f32[720,320]{0,1:T(8,128)} %param.15) | copy-start | bytes 2764804
  67.9 0.7 copy-start.7
  67.9 0.7 copy-start.6
  68.6 1.1 %copy-start.3 = (bf16[8,320,128]{2,1,0:T(8,128)(2,1)S(1)}, bf16[8,320,128]{2,1,0:T(8,128)(2,1)}, u32[]{:S(2)}) copy-start(bf16[8,320,128]{2,1,0:T(8,128)(2,1)} %get-tuple-element.21.act_ref) | copy-start | bytes 1966084
  69.7 1.1 %copy-start.4 = (bf16[8,320,128]{2,1,0:T(8,128)(2,1)S(1)}, bf16[8,320,128]{2,1,0:T(8,128)(2,1)}, u32[]{:S(2)}) copy-start(bf16[8,320,128]{2,1,0:T(8,128)(2,1)} %get-tuple-element.22.ig_ref) | copy-start | bytes 1966084
  70.8 1.0 %copy-start.5 = (bf16[320,720]{1,0:T(8,128)(2,1)S(1)}, bf16[320,720]{1,0:T(8,128)(2,1)}, u32[]{:S(2)}) copy-start(bf16[320,720]{1,0:T(8,128)(2,1)} %get-tuple-element.23.grad_ref) | copy-start | bytes 1382404

commit v4 on v3

--- a/solution.py
+++ b/solution.py
@@ -317,20 +317,12 @@
     hs2[1] = g1[jnp.clip(live - 1, 0, slots - 1)]
     halo_start(hs2, hr2, h2_s, h2_r)
 
-    for b in range(3):
-        right = g1[...].reshape(cells, chan) if b == 1 else (g0 if b == 0 else g2)[...]
-        wide[...] = jnp.dot(xcat_t[...], right, preferred_element_type=F32)
-        if aligned:
-            for fi, p, low, size, tap, at in pieces:
-                if tap % 3 == b:
-                    a = tap // 3
-                    dwbuf[fi, p // 2, p % 2, low:low + size, :] = wide[
-                        a * chan + at:a * chan + at + size, :
-                    ].astype(BF16)
-        else:
-            for a in range(3):
-                dwf[(3 * a + b) * chan:(3 * a + b + 1) * chan, :] = wide[a * chan:(a + 1) * chan, :]
-    for fi in range(shards):
+    def sibling_copy(fi):
+        return copy(
+            dwbuf.at[fi, :, 1 - c], sbuf.at[fi], b_s.at[fi], b_r.at[fi], sibling, f
+        )
+
+    def finish_shard(fi):
         for p in range(tiles):
             low, high = p * part, min(shard, (p + 1) * part)
             if high <= low:
@@ -342,18 +334,40 @@
                 dwbuf[fi, p // 2, p % 2] = rows.astype(BF16)
             elif high - low < part:
                 dwbuf[fi, p // 2, p % 2, high - low:part, :] = jnp.zeros((part - high + low, chan), BF16)
-
-    order = list(range(1, shards)) + [0]
-    for k in order:
-        fd = lax.rem(f + k, shards)
-        push(dwbuf.at[fd, :, 1 - c], sbuf.at[k], b_s.at[k], b_r.at[k], sibling, f)
-    for k in order:
-        fd = lax.rem(f + k, shards)
-        copy(sbuf.at[k], sbuf.at[k], b_s.at[k], b_r.at[k], sibling, f).wait_recv()
+        made = sibling_copy(fi)
+        made.start()
+        sent.append(made)
+
+    def plane_send(fi):
+        sibling_copy(fi).wait_recv()
         for j in range(1, chips):
             to = peer_chip(j)
-            pbuf[k, j - 1] = (dwbuf[fd, to, c].astype(F32) + sbuf[k, to].astype(F32)).astype(BF16)
-            push(pbuf.at[k, j - 1], qbuf.at[k, j - 1], q_s.at[k, j - 1], q_r.at[k, j - 1], to * 2 + c, f)
+            pbuf[fi, j - 1] = (dwbuf[fi, to, c].astype(F32) + sbuf[fi, to].astype(F32)).astype(BF16)
+            push(pbuf.at[fi, j - 1], qbuf.at[fi, j - 1], q_s.at[fi, j - 1], q_r.at[fi, j - 1], to * 2 + c, f)
+
+    done, passed = 0, 0
+    for a in range(3):
+        left = xcat_t[a * chan:(a + 1) * chan, :]
+        for b in range(3):
+            right = g1[...].reshape(cells, chan) if b == 1 else (g0 if b == 0 else g2)[...]
+            block = jnp.dot(left, right, preferred_element_type=F32)
+            if aligned:
+                wide[...] = block
+                for fi, p, low, size, tap, at in pieces:
+                    if tap == 3 * a + b:
+                        dwbuf[fi, p // 2, p % 2, low:low + size, :] = wide[at:at + size, :].astype(BF16)
+            else:
+                dwf[(3 * a + b) * chan:(3 * a + b + 1) * chan, :] = block
+        ready = done
+        while done < shards and (done + 1) * shard <= 3 * (a + 1) * chan:
+            finish_shard(done)
+            done += 1
+        while passed < ready:
+            plane_send(passed)
+            passed += 1
+    while passed < shards:
+        plane_send(passed)
+        passed += 1
 
     halo_wait(hs2, hr2, h2_s, h2_r)
     grad_below = hr2[1].astype(F32)
@@ -378,23 +392,27 @@
     ig_out = pltpu.make_async_copy(ig_ref, ig_any, loc.at[2])
     ig_out.start()
 
-    own = None
-    for k in order:
-        fd = lax.rem(f + k, shards)
-        summed = dwbuf[fd, ch, c].astype(F32) + sbuf[k, ch].astype(F32)
+    def shard_copy(fi):
+        return copy(zbuf.at[fi], rbuf.at[f], r_s.at[fi], r_r.at[f], t, fi)
+
+    for fi in range(shards):
+        summed = dwbuf[fi, ch, c].astype(F32) + sbuf[fi, ch].astype(F32)
         for j in range(1, chips):
-            block = qbuf.at[k, j - 1]
-            copy(block, block, q_s.at[k, j - 1], q_r.at[k, j - 1], t, f).wait_recv()
-            summed = summed + qbuf[k, j - 1].astype(F32)
-        if k == 0:
-            own = summed
-        else:
-            zbuf[k - 1] = summed.astype(BF16)
-            push(zbuf.at[k - 1], rbuf.at[k - 1], r_s.at[k - 1], r_r.at[k - 1], t, fd)
-    for k in range(1, shards):
-        block = rbuf.at[k - 1]
-        copy(block, block, r_s.at[k - 1], r_r.at[k - 1], t, f).wait_recv()
-        own = own + rbuf[k - 1].astype(F32)
+            block = qbuf.at[fi, j - 1]
+            copy(block, block, q_s.at[fi, j - 1], q_r.at[fi, j - 1], t, f).wait_recv()
+            summed = summed + qbuf[fi, j - 1].astype(F32)
+        zbuf[fi] = summed.astype(BF16)
+
+        @pl.when(f != fi)
+        def _():
+            shard_copy(fi).start()
+
+    own = zbuf[f].astype(F32)
+    for k in range(1, shards):
+        fs = lax.rem(f + k, shards)
+        block = rbuf.at[fs]
+        copy(block, block, r_s.at[fs], r_r.at[fs], t, f).wait_recv()
+        own = own + rbuf[fs].astype(F32)
     fbuf[t] = own.astype(BF16)
     mine = fbuf.at[t]
     for j in range(1, chips):
@@ -423,6 +441,12 @@
         low, high = p * part, min(shard, (p + 1) * part)
         wrow[low:high, :] = fbuf[p].astype(F32)[:high - low]
     wg_ref[...] = wrow[...].T.astype(BF16)
+
+    for fi in range(shards):
+
+        @pl.when(f != fi)
+        def _():
+            shard_copy(fi).wait_send()
 
     act_out.wait()
     ig_out.wait()
@@ -490,7 +514,7 @@
             pltpu.VMEM((shards, tiles, part, chan), BF16),
             pltpu.VMEM((3, 3 * chan, chan), BF16),
             pltpu.VMEM((3, 3 * chan, chan), BF16),
-            pltpu.VMEM((3 * chan, chan), F32),
+            pltpu.VMEM((chan, chan), F32),
             pltpu.VMEM((cells, 3 * chan), BF16),
             pltpu.VMEM((3 * chan, cells), BF16),
             pltpu.VMEM((cells, 3 * chan), BF16),
@@ -513,8 +537,8 @@
             pltpu.VMEM((shards, chips, part, chan), BF16),
             pltpu.VMEM((shards, chips - 1, part, chan), BF16),
             pltpu.VMEM((shards, chips - 1, part, chan), BF16),
-            pltpu.VMEM((shards - 1, part, chan), BF16),
-            pltpu.VMEM((shards - 1, part, chan), BF16),
+            pltpu.VMEM((shards, part, chan), BF16),
+            pltpu.VMEM((shards, part, chan), BF16),
             pltpu.VMEM((tiles, part, chan), BF16),
             dma((shards - 1,)), dma((shards - 1,)),
             dma((shards - 1, chips - 1)), dma((shards - 1, chips - 1)),
@@ -525,7 +549,7 @@
             dma((shards - 1,)), dma((shards - 1,)),
             dma((shards,)), dma((shards,)),
             dma((shards, chips - 1)), dma((shards, chips - 1)),
-            dma((shards - 1,)), dma((shards - 1,)),
+            dma((shards,)), dma((shards,)),
             dma((chips - 1,)), dma((chips - 1,)),
             dma((chips,)), dma((chips,)),
         ],
@@ -552,7 +576,7 @@
         out_shape=(picture, picture, rows_out, rows_out, rows_out, rows_out, line, line),
         in_specs=[slab, slab, strip, strip, strip, strip, whole, whole],
         out_specs=(slab, slab, strip, strip, strip, strip, whole, whole),
-        compiler_params=pltpu.CompilerParams(vmem_limit_bytes=32 * 2**20),
+        compiler_params=pltpu.CompilerParams(vmem_limit_bytes=58 * 2**20),
         name="adam_step",
     )(act, ig, wg, master_weight.T, first_moment.T, second_moment.T, gg, bg)
     act, ig = swapped(act).reshape(images.shape), swapped(ig).reshape(images.shape)

time: 75 us -> 73.4 us (0.979)
  the two profiles are of different devices: /device:TPU:1 before, /device:TPU:25 now
where the time goes in v4:
time: 73.4 us; the launch traced here: 73.1 us
  Pallas kernels  71.8 us (98%)
  between operations  1.29 us (2%)
    pallas_call x1, Pallas kernels, local(): pl.pallas_call(functools.partial(kernel, tiles, shards, part), out_shape=...  66.5 us
    pallas_call x1, Pallas kernels, local(): pl.pallas_call(functools.partial(adam, scale), grid=(steps,), out_shape=(...  5.37 us

profile of v4, /device:TPU:25, one launch (start us, length us, event | category | flops | bytes accessed | tf_op | source)
XLA Modules:
  0.0 73.1 jit_solution(11884619607674177162)
XLA Ops:
  1.3 66.5 %conv_block.1 = (bf16[8,320,128]{2,1,0:T(8,128)(2,1)}, bf16[8,320,128]{2,1,0:T(8,128)(2,1)}, bf16[320,720]{1,0:T(8,128)(2,1)}, f32[320]{0:T(512)}, f32[320]{0:T(512)}) custom-call(s32[1,1]{1,0:T(1,128)S(6)} %copy.16.rows_ref, bf16[8,320,128]{2,1,0:T(8,128)(2,1)} %bitcast.27, bf16[8,320,128]{2,1,0:T(8,128)(2,1)} %bitcast.28, f32[320,720]{1,0:T(8,128)} %bitcast.19, ...), custom_call_target="tpu_custom_call" | custom-call | flops 5662310400 | bytes 16777216 | tf_op jit(solution)/shard_map/conv_block/pallas_call | solution.py:500
  67.7 5.4 %adam_step.1 = (bf16[8,320,128]{2,1,0:T(8,128)(2,1)}, bf16[8,320,128]{2,1,0:T(8,128)(2,1)}, f32[320,720]{1,0:T(8,128)}, f32[320,720]{1,0:T(8,128)}, f32[320,720]...) custom-call(bf16[8,320,128]{2,1,0:T(8,128)(2,1)} %get-tuple-element.21.act_ref, ...), custom_call_target="tpu_custom_call" | custom-call | tf_op jit(solution)/shard_map/adam_step/pallas_call | solution.py:573
